TPU v7x, 32 devices: a whole 2x2x4 slice. The times are simulated.
32 devices in a mesh: groups: 2 (over y), dp: 1, expert: 16 (over z, x, core).
Axes of the slice: x: 2, y: 2, z: 4, core: 2. Of those that a mesh axis runs over, the one named last changes fastest.
Arguments:
- student_input: bfloat16 [4096, 1024], P(('groups', 'dp', 'expert')), parts along dimension 0, may hold values from -6 to 6
- judge_output: bfloat16 [4096, 1024], P(('groups', 'dp', 'expert')), parts along dimension 0, may hold values from -4 to 4
- expert_ids: int32 [4096, 8], P(('groups', 'dp', 'expert')), parts along dimension 0, may hold values from 0 to 15, all different within a row; in each aligned block of 128 rows (0 to 127, 128 to 255, ...) at most 80 rows name the same one
- route_weights: float32 [4096, 8], P(('groups', 'dp', 'expert')), parts along dimension 0, may hold values from 0.02 to 0.3
- w_gate: bfloat16 [16, 384, 1024], P('expert', 'dp'), may hold values from -0.1875 to 0.1875
- w_up: bfloat16 [16, 384, 1024], P('expert', 'dp'), may hold values from -0.1875 to 0.1875
- w_down: bfloat16 [16, 384, 1024], P('expert', 'dp'), may hold values from -0.3125 to 0.3125
Outputs:
- student_output: bfloat16 [4096, 1024], P(('groups', 'dp', 'expert')), parts along dimension 0
- route_grads: float32 [4096, 8], P(('groups', 'dp', 'expert')), parts along dimension 0
- grad_gate: bfloat16 [32, 384, 1024], P(('groups', 'expert'), 'dp'), parts along dimension 0
- grad_up: bfloat16 [32, 384, 1024], P(('groups', 'expert'), 'dp'), parts along dimension 0
- grad_down: bfloat16 [32, 384, 1024], P(('groups', 'expert'), 'dp'), parts along dimension 0
There are 2 independent parts, one for each index of `groups`. A program takes and returns all parts, laid end to end along the dimension named above; an argument that names none is the same for every part. Nothing has to cross between parts.
Inputs may be any that keep to these rules, and one draw needn't show every extreme that they name: `expert_ids`: each token names 8 different experts; among the 128 tokens of one device (aligned blocks of rows) no expert is named more than 80 times.
All inputs are finite; a program needn't handle non-finite values.
Results may differ from a plain program's by a relative error of at most 0.0075.
Values may be sent and summed in bfloat16 or wider, within the bound.
A program may use at most 64 MiB of HBM per device.

v0:
```python
import math

import jax
import jax.numpy as jnp
from jax import lax
from jax.sharding import PartitionSpec as P


def slot_layout(flat_ids, experts, capacity):
    pick_total = flat_ids.shape[0]
    span = math.gcd(pick_total, 128)
    count_blocks = pick_total // span
    onehot = (flat_ids[:, None] == jnp.arange(experts, dtype=jnp.int32)[None, :]).astype(
        jnp.bfloat16
    )
    onehot = onehot.reshape(count_blocks, span, experts)
    rows_here = jnp.arange(span, dtype=jnp.int32)
    lower = (rows_here[:, None] > rows_here[None, :]).astype(jnp.bfloat16)
    within = jnp.einsum("ij,bje->bie", lower, onehot, preferred_element_type=jnp.float32)
    totals = jnp.sum(onehot.astype(jnp.float32), axis=1)
    before = jnp.cumsum(totals, axis=0) - totals
    earlier = within + before[:, None, :]
    slot_index = jnp.sum(earlier * onehot.astype(jnp.float32), axis=2).reshape(-1).astype(jnp.int32)
    position = flat_ids * capacity + slot_index
    source = (
        jnp.zeros((experts * capacity,), jnp.int32)
        .at[position]
        .set(jnp.arange(1, pick_total + 1, dtype=jnp.int32))
    )
    return (position, source)


def hidden_units(row_block, gate_full, up_full):
    gate_pre = jnp.einsum("esd,efd->esf", row_block, gate_full, preferred_element_type=jnp.float32)
    up_pre = jnp.einsum("esd,efd->esf", row_block, up_full, preferred_element_type=jnp.float32)
    hidden = (gate_pre * jax.nn.sigmoid(gate_pre) * up_pre).astype(jnp.bfloat16)
    return (gate_pre, up_pre, hidden)


def on_device(student_input, judge_output, expert_ids, route_weights, w_gate, w_up, w_down):
    tok_count, dim_model = student_input.shape
    top_picks = expert_ids.shape[1]
    exp_local = w_gate.shape[0]
    senders = lax.axis_size("expert")
    experts = exp_local * senders
    capacity = min(tok_count, tok_count * top_picks * 5 // (4 * experts))
    flat_ids = expert_ids.reshape(-1)
    position, source = slot_layout(flat_ids, experts, capacity)
    is_valid = (source > 0)[:, None]
    pick_index = jnp.maximum(source - 1, 0)
    empty_rows = jnp.zeros((), jnp.bfloat16)
    send_rows = jnp.where(is_valid, student_input[pick_index // top_picks], empty_rows).reshape(
        experts, capacity, dim_model
    )
    gate_full, up_full, down_full = (
        lax.all_gather(w_gate, "dp", axis=1, tiled=True),
        lax.all_gather(w_up, "dp", axis=1, tiled=True),
        lax.all_gather(w_down, "dp", axis=1, tiled=True),
    )
    row_block = lax.all_to_all(send_rows, "expert", split_axis=0, concat_axis=1, tiled=True)
    gate_pre, up_pre, hidden = hidden_units(row_block, gate_full, up_full)
    expert_out = jnp.einsum(
        "esf,efd->esd", hidden, down_full, preferred_element_type=jnp.float32
    ).astype(jnp.bfloat16)
    returned = lax.all_to_all(
        expert_out, "expert", split_axis=1, concat_axis=0, tiled=True
    ).reshape(experts * capacity, dim_model)
    pick_out = returned[position].reshape(tok_count, top_picks, dim_model)
    pick_wide = pick_out.astype(jnp.float32)
    mixture = jnp.sum(route_weights[:, :, None] * pick_wide, axis=1)
    residual = mixture - judge_output.astype(jnp.float32)
    route_grads = jnp.sum(pick_wide * residual[:, None, :], axis=2)
    out_grad = (
        (route_weights[:, :, None] * residual[:, None, :])
        .astype(jnp.bfloat16)
        .reshape(tok_count * top_picks, dim_model)
    )
    send_grads = jnp.where(is_valid, out_grad[pick_index], empty_rows).reshape(
        experts, capacity, dim_model
    )
    grad_block = lax.all_to_all(send_grads, "expert", split_axis=0, concat_axis=1, tiled=True)
    hidden_grad = jnp.einsum(
        "esd,efd->esf", grad_block, down_full, preferred_element_type=jnp.float32
    )
    sig_gate = jax.nn.sigmoid(gate_pre)
    gate_grad = (hidden_grad * up_pre * sig_gate * (1.0 + gate_pre * (1.0 - sig_gate))).astype(
        jnp.bfloat16
    )
    up_grad = (hidden_grad * gate_pre * sig_gate).astype(jnp.bfloat16)
    gate_part = jnp.einsum("esf,esd->efd", gate_grad, row_block, preferred_element_type=jnp.float32)
    up_part = jnp.einsum("esf,esd->efd", up_grad, row_block, preferred_element_type=jnp.float32)
    down_part = jnp.einsum("esf,esd->efd", hidden, grad_block, preferred_element_type=jnp.float32)
    grad_gate, grad_up, grad_down = (
        lax.psum_scatter(
            gate_part.astype(jnp.bfloat16), "dp", scatter_dimension=1, tiled=True
        ).astype(jnp.float32),
        lax.psum_scatter(
            up_part.astype(jnp.bfloat16), "dp", scatter_dimension=1, tiled=True
        ).astype(jnp.float32),
        lax.psum_scatter(
            down_part.astype(jnp.bfloat16), "dp", scatter_dimension=1, tiled=True
        ).astype(jnp.float32),
    )
    return (
        mixture.astype(jnp.bfloat16),
        route_grads,
        grad_gate.astype(jnp.bfloat16),
        grad_up.astype(jnp.bfloat16),
        grad_down.astype(jnp.bfloat16),
    )


def solution(mesh):
    placed = (
        P(("groups", "dp", "expert"), None),
        P(("groups", "dp", "expert"), None),
        P(("groups", "dp", "expert"), None),
        P(("groups", "dp", "expert"), None),
        P("expert", "dp", None),
        P("expert", "dp", None),
        P("expert", "dp", None),
    )
    return jax.shard_map(
        on_device,
        mesh=mesh,
        in_specs=placed,
        out_specs=(
            P(("groups", "dp", "expert"), None),
            P(("groups", "dp", "expert"), None),
            P(("groups", "expert"), "dp", None),
            P(("groups", "expert"), "dp", None),
            P(("groups", "expert"), "dp", None),
        ),
        check_vma=False,
    )
```

profile of v0, /device:TPU:11, one launch (start us, length us, event | category | flops | bytes accessed | tf_op | source)
XLA Modules:
  0.0 291.6 jit_solution(2452623419388425537)
XLA Ops:
  0.6 0.0 copy-start
  0.6 0.0 copy-start.1
  0.7 0.8 broadcast_multiply_fusion
  1.4 0.8 copy.25
  2.2 0.1 copy.24
  2.3 0.1 mul.90
  2.4 0.1 eq.17
  2.5 0.1 convert_reduce_fusion
  2.6 0.2 fusion.9
  2.9 4.3 %scatter_custom_fusion = s32[1280]{0:T(1024)S(1)} fusion(s32[1024]{0:T(1024)S(1)} %bitcast.68, s32[1024]{0:T(1024)S(1)} %iota_add_fusion, s32[]{:T(128)} %constant.15.clone.1), kind=kCustom, calls=%fused_computation.54 | custom fusion | bytes 5124 | tf_op jit(solution)/shard_map/scatter | solution.py:28
  7.2 0.1 broadcast_in_dim.35
  7.3 0.0 copy-done.1
  7.3 5.1 %gather_fusion = bf16[1280,1024]{1,0:T(8,128)(2,1)} fusion(bf16[128,1024]{1,0:T(8,128)(2,1)S(1)} %copy-done.1, s32[2048]{0:T(1024)S(1)} %get-tuple-element.22), kind=kCustom, calls=%fused_computation | custom fusion | bytes 5248000 | tf_op jit(solution)/shard_map/gather | solution.py:52
  12.4 2.0 broadcast_select_fusion.1
  14.4 0.0 copy-start.9
  14.4 65.0 %all_to_all.12 = bf16[16,80,1024]{2,1,0:T(8,128)(2,1)S(1)} all-to-all(bf16[16,80,1024]{2,1,0:T(8,128)(2,1)S(1)} %broadcast_select_fusion.1), channel_id=1, replica_groups=mesh['groups'=2,'dp'=1,'expert'=16] {'expert'}, dimensions={0} | all-to-all | bytes 5242880 | tf_op jit(solution)/shard_map/all_to_all | solution.py:60
  79.4 0.0 copy-start.3
  79.4 0.0 copy-done.9
  79.4 0.0 copy-start.10
  79.4 1.5 fusion.15
  81.0 0.0 copy-done.3
  81.0 0.1 copy-done.10
  81.1 0.0 copy-start.11
  81.1 3.0 %multiply_convert_fusion.2 = (bf16[1280,384]{1,0:T(8,128)(2,1)S(1)}, f32[1280,384]{1,0:T(8,128)}) fusion(f32[1280,384]{1,0:T(8,128)S(1)} %fusion.15, bf16[1280,1024]{1,0:T(8,128)(2,1)S(1)} %bitcast.65, bf16[1,384,1024]{2,1,0:T(8,128)(2,1)S(1)} %copy-done.10), kind=kOutput, calls=%fused_computation.17 | convolution fusion | flops 1009582080 | bytes 8323072 | tf_op jit(solution)/shard_map/esd,efd->esf/dot_general | solution.py:35
  84.1 0.0 copy-done.11
  84.1 0.0 copy-start.5
  84.1 0.0 copy-done
  84.1 1.5 fusion.3
  85.7 0.0 copy-done.5
  85.7 18.2 %copy.33 = bf16[1,1280,1024]{2,0,1:T(2,128)(2,1)} copy(bf16[1,1280,1024]{2,1,0:T(8,128)(2,1)S(1)} %fusion.3) | data formatting | bytes 5242880 | tf_op jit(solution)/shard_map/convert_element_type | solution.py:64
  103.9 0.5 broadcast.108
  104.4 15.6 %reduce.4 = bf16[1280,1024]{1,0:T(8,128)(2,1)S(1)} reduce(bf16[1280,1,1024]{2,1,0:T(2,128)(2,1)} %bitcast.60, bf16[]{:T(256)} %broadcast.108), dimensions={1}, to_apply=%bitcast.58.reduce_sub_computation | reduce | bytes 5242882
  120.0 3.1 %reshape.225 = bf16[16,2,40960]{2,1,0:T(2,128)(2,1)} reshape(bf16[1280,1024]{1,0:T(8,128)(2,1)S(1)} %reduce.4) | data formatting | bytes 5242880
  123.1 0.0 copy-start.8
  123.1 5.3 %all-to-all-start.1 = ((bf16[16,2,40960]{2,1,0:T(2,128)(2,1)}), bf16[16,2,40960]{2,1,0:T(2,128)(2,1)S(1)}, u32[]{:S(2)}, u32[]{:S(2)}) async-start(bf16[16,2,40960]{2,1,0:T(2,128)(2,1)} %reshape.225), calls=%async_computation.1 | async-start | bytes 5242880 | tf_op jit(solution)/shard_map/all_to_all | solution.py:65
  128.4 0.0 copy-done.8
  128.4 0.1 copy.23
  128.5 0.1 mul.97
  128.6 58.4 %all-to-all-done.1 = bf16[16,2,40960]{2,1,0:T(2,128)(2,1)S(1)} async-done(((bf16[16,2,40960]{2,1,0:T(2,128)(2,1)}), bf16[16,2,40960]{2,1,0:T(2,128)(2,1)S(1)}, u32[]{:S(2)}, u32[]{:S(2)}) %all-to-all-start.1) | async-done | bytes 2621472 | tf_op jit(solution)/shard_map/all_to_all | solution.py:65
  187.1 7.2 %reshape.226 = bf16[1280,1,1024]{2,1,0:T(2,128)(2,1)} reshape(bf16[16,2,40960]{2,1,0:T(2,128)(2,1)S(1)} %all-to-all-done.1) | data formatting | bytes 5242880
  194.2 3.5 %copy.32 = bf16[1,1280,1024]{2,1,0:T(8,128)(2,1)S(1)} copy(bf16[1,1280,1024]{2,0,1:T(2,128)(2,1)} %bitcast.61) | data formatting | bytes 5242880
  197.8 5.4 %gather_fusion.1 = bf16[1024,1024]{1,0:T(8,128)(2,1)} fusion(bf16[1280,1024]{1,0:T(8,128)(2,1)S(1)} %bitcast.59, s32[1024]{0:T(1024)S(1)} %broadcast_clamp_fusion), kind=kCustom, calls=%fused_computation.1 | custom fusion | bytes 4198400 | tf_op jit(solution)/shard_map/gather | solution.py:68
  203.2 0.0 copy-start.7
  203.2 3.0 %fusion = f32[128,1024]{1,0:T(8,128)S(1)} fusion(bf16[1024,1024]{1,0:T(8,128)(2,1)} %gather_fusion.1, f32[128,8]{1,0:T(8,128)S(1)} %copy.23), kind=kLoop, calls=%fused_computation.6 | loop fusion | flops 3014656 | bytes 2625536 | tf_op jit(solution)/shard_map/reduce_sum | solution.py:70
  206.1 0.0 copy-done.7
  206.1 0.8 convert_subtract_fusion
  206.9 0.3 fusion.2
  207.2 5.1 %gather_fusion.2 = bf16[1280,1024]{1,0:T(8,128)(2,1)} fusion(bf16[1024,1024]{1,0:T(8,128)(2,1)S(1)} %fusion.2, s32[2048]{0:T(1024)S(1)} %get-tuple-element.21), kind=kCustom, calls=%fused_computation.2 | custom fusion | bytes 5248000 | tf_op jit(solution)/shard_map/gather | solution.py:78
  212.3 3.5 %broadcast_select_fusion = bf16[16,80,1024]{2,1,0:T(8,128)(2,1)} fusion(bf16[16,80,1024]{2,1,0:T(8,128)(2,1)} %bitcast.62, pred[16,80]{1,0:T(8,128)(4,1)S(1)} %broadcast_in_dim.35), kind=kLoop, calls=%fused_computation.13 | loop fusion | flops 1310720 | bytes 5244160 | tf_op jit(solution)/shard_map/jit(_where)/select_n | solution.py:78
  215.8 0.0 copy-start.2
  215.8 5.0 %all-to-all-start.2 = ((bf16[16,80,1024]{2,1,0:T(8,128)(2,1)}), bf16[16,80,1024]{2,1,0:T(8,128)(2,1)}, u32[]{:S(2)}, u32[]{:S(2)}) async-start(bf16[16,80,1024]{2,1,0:T(8,128)(2,1)} %broadcast_select_fusion), calls=%async_computation.2 | async-start | bytes 5242880 | tf_op jit(solution)/shard_map/all_to_all | solution.py:81
  220.8 0.0 copy-done.2
  220.8 0.5 fusion.1
  221.3 0.7 copy.28
  222.0 57.6 %all-to-all-done.2 = bf16[16,80,1024]{2,1,0:T(8,128)(2,1)} async-done(((bf16[16,80,1024]{2,1,0:T(8,128)(2,1)}), bf16[16,80,1024]{2,1,0:T(8,128)(2,1)}, u32[]{:S(2)}, u32[]{:S(2)}) %all-to-all-start.2) | async-done | bytes 2621472 | tf_op jit(solution)/shard_map/all_to_all | solution.py:81
  279.6 3.4 %fusion.10 = f32[1280,384]{1,0:T(8,128)S(1)} fusion(bf16[1280,1024]{1,0:T(8,128)(2,1)} %bitcast.14, bf16[1,384,1024]{2,1,0:T(8,128)(2,1)S(1)} %copy-done), kind=kOutput, calls=%fused_computation.29 | convolution fusion | flops 1006632960 | bytes 5373952 | tf_op jit(solution)/shard_map/esd,efd->esf/dot_general | solution.py:82
  283.1 0.0 copy-done.6
  283.1 0.0 copy-start.4
  283.1 4.0 %fusion.6 = bf16[1,384,1024]{2,1,0:T(8,128)(2,1)} fusion(bf16[1280,384]{1,0:T(8,128)(2,1)S(1)} %copy-done.6, bf16[1280,1024]{1,0:T(8,128)(2,1)} %bitcast.14), kind=kOutput, calls=%fused_computation.24 | convolution fusion | flops 1007026176 | bytes 4390912 | tf_op jit(solution)/shard_map/esf,esd->efd/dot_general | solution.py:92
  287.1 0.0 copy-done.12
  287.1 0.0 copy-done.4
  287.1 2.2 fusion.5
  289.2 0.0 copy-done.13
  289.2 2.4 fusion.4
  (12 shorter events, 0.1 us)
Async XLA Ops:
  0.6 83.5 %copy-start = (bf16[1,384,1024]{2,1,0:T(8,128)(2,1)S(1)}, bf16[1,384,1024]{2,1,0:T(8,128)(2,1)}, u32[]{:S(2)}) copy-start(bf16[1,384,1024]{2,1,0:T(8,128)(2,1)} %param.13) | copy-start | bytes 2359300
  0.6 6.7 %copy-start.1 = (bf16[128,1024]{1,0:T(8,128)(2,1)S(1)}, bf16[128,1024]{1,0:T(8,128)(2,1)}, u32[]{:S(2)}) copy-start(bf16[128,1024]{1,0:T(8,128)(2,1)} %param.7) | copy-start | bytes 786436
  14.4 65.0 %copy-start.9 = (bf16[1,384,1024]{2,1,0:T(8,128)(2,1)S(1)}, bf16[1,384,1024]{2,1,0:T(8,128)(2,1)}, u32[]{:S(2)}) copy-start(bf16[1,384,1024]{2,1,0:T(8,128)(2,1)} %param.11) | copy-start | bytes 2359300
  79.4 1.6 copy-start.3
  79.4 1.7 copy-start.10
  81.1 3.0 %copy-start.11 = (f32[1280,384]{1,0:T(8,128)}, f32[1280,384]{1,0:T(8,128)S(1)}, u32[]{:S(2)}) copy-start(f32[1280,384]{1,0:T(8,128)S(1)} %fusion.15) | copy-start | bytes 5898244
  84.1 1.5 copy-start.5
  123.1 5.3 %copy-start.8 = (f32[128,8]{0,1:T(8,128)S(1)}, f32[128,8]{0,1:T(8,128)}, u32[]{:S(2)}) copy-start(f32[128,8]{0,1:T(8,128)} %param.10) | copy-start | bytes 12292
  123.1 64.0 %all-to-all-start.1 = ((bf16[16,2,40960]{2,1,0:T(2,128)(2,1)}), bf16[16,2,40960]{2,1,0:T(2,128)(2,1)S(1)}, u32[]{:S(2)}, u32[]{:S(2)}) async-start(bf16[16,2,40960]{2,1,0:T(2,128)(2,1)} %reshape.225), calls=%async_computation.1 | async-start | bytes 5242880 | tf_op jit(solution)/shard_map/all_to_all | solution.py:65
  203.2 3.0 %copy-start.7 = (bf16[128,1024]{1,0:T(8,128)(2,1)S(1)}, bf16[128,1024]{1,0:T(8,128)(2,1)}, u32[]{:S(2)}) copy-start(bf16[128,1024]{1,0:T(8,128)(2,1)} %param.8) | copy-start | bytes 786436
  215.8 5.0 %copy-start.2 = (bf16[1024,1024]{1,0:T(8,128)(2,1)S(1)}, bf16[1024,1024]{1,0:T(8,128)(2,1)}, u32[]{:S(2)}) copy-start(bf16[1024,1024]{1,0:T(8,128)(2,1)} %gather_fusion.1) | copy-start | bytes 6291460
  215.8 63.8 %all-to-all-start.2 = ((bf16[16,80,1024]{2,1,0:T(8,128)(2,1)}), bf16[16,80,1024]{2,1,0:T(8,128)(2,1)}, u32[]{:S(2)}, u32[]{:S(2)}) async-start(bf16[16,80,1024]{2,1,0:T(8,128)(2,1)} %broadcast_select_fusion), calls=%async_computation.2 | async-start | bytes 5242880 | tf_op jit(solution)/shard_map/all_to_all | solution.py:81
  279.6 3.5 %copy-start.6 = (bf16[1280,384]{1,0:T(8,128)(2,1)S(1)}, bf16[1280,384]{1,0:T(8,128)(2,1)}, u32[]{:S(2)}) copy-start(bf16[1280,384]{1,0:T(8,128)(2,1)} %copy-done.5) | copy-start | bytes 2949124
  279.6 7.5 %copy-start.12 = (f32[1280,384]{1,0:T(8,128)S(1)}, f32[1280,384]{1,0:T(8,128)}, u32[]{:S(2)}) copy-start(f32[1280,384]{1,0:T(8,128)} %copy-done.11) | copy-start | bytes 5898244
  283.1 4.0 %copy-start.4 = (bf16[16,80,1024]{2,1,0:T(8,128)(2,1)S(1)}, bf16[16,80,1024]{2,1,0:T(8,128)(2,1)}, u32[]{:S(2)}) copy-start(bf16[16,80,1024]{2,1,0:T(8,128)(2,1)} %copy-done.3) | copy-start | bytes 7864324
  287.1 2.2 copy-start.13
where the time goes:
time: 292 us
  waiting for transfers between devices  116 us (40%)
  blocking collectives  65 us (22%)
  local copies, waits for them, and re-layouts  54.6 us (19%)
  other arithmetic  26.5 us (9%)
  matrix products  18.2 us (6%)
  starting transfers between devices  10.3 us (4%)
    all_to_all x1, blocking collectives, on_device(): lax.all_to_all(send_rows, 'expert', split_axis=0, concat_axis=1, tiled=True)  65 us
    all_to_all x1, waiting for transfers between devices, on_device(): lax.all_to_all(expert_out, 'expert', split_axis=1, concat_axis=0, tiled=T...  58.4 us
    all_to_all x1, waiting for transfers between devices, on_device(): lax.all_to_all(send_grads, 'expert', split_axis=0, concat_axis=1, tiled=T...  57.6 us
    convert_element_type x1, local copies, waits for them, and re-layouts, on_device(): expert_out = jnp.einsum('esf,efd->esd', hidden, down_full, preferred_elem...  18.2 us
    unnamed x35, local copies, waits for them, and re-layouts  16.1 us
    unnamed x1, other arithmetic  15.6 us
  transfers between devices with their start and end apart: 2, of which 2 were waited for; matrix products, arithmetic and copies ran while one was open for 0% of the time, Pallas kernels for 0%

commit v1 on v0

--- a/solution.py
+++ b/solution.py
@@ -37,7 +37,7 @@
     return (gate_pre, up_pre, hidden)
 
 
-def on_device(student_input, judge_output, expert_ids, route_weights, w_gate, w_up, w_down):
+def routed_rows(student_input, judge_output, expert_ids, route_weights, w_gate, w_up, w_down):
     tok_count, dim_model = student_input.shape
     top_picks = expert_ids.shape[1]
     exp_local = w_gate.shape[0]
@@ -110,6 +110,71 @@
     )
 
 
+def dense_rows(student_input, judge_output, expert_ids, route_weights, w_gate, w_up, w_down):
+    senders = lax.axis_size("expert")
+    exp_local = w_gate.shape[0]
+    experts = exp_local * senders
+    tok_count, dim_model = student_input.shape
+    gate_full, up_full, down_full = (
+        lax.all_gather(w_gate, "dp", axis=1, tiled=True),
+        lax.all_gather(w_up, "dp", axis=1, tiled=True),
+        lax.all_gather(w_down, "dp", axis=1, tiled=True),
+    )
+    chosen = expert_ids[:, :, None] == jnp.arange(experts, dtype=jnp.int32)[None, None, :]
+    dense_weights = jnp.sum(jnp.where(chosen, route_weights[:, :, None], 0.0), axis=1)
+    rows = lax.all_gather(student_input, "expert", axis=0, tiled=True)
+    weights_here = lax.all_to_all(
+        dense_weights.T.reshape(senders, exp_local, tok_count),
+        "expert",
+        split_axis=0,
+        concat_axis=0,
+        tiled=True,
+    )
+    weights_here = weights_here.transpose(1, 0, 2).reshape(exp_local, senders * tok_count, 1)
+    gate_pre = jnp.einsum("sd,efd->esf", rows, gate_full, preferred_element_type=jnp.float32)
+    up_pre = jnp.einsum("sd,efd->esf", rows, up_full, preferred_element_type=jnp.float32)
+    sig_gate = jax.nn.sigmoid(gate_pre)
+    hidden = (gate_pre * sig_gate * up_pre).astype(jnp.bfloat16)
+    expert_out = jnp.einsum(
+        "esf,efd->esd", hidden, down_full, preferred_element_type=jnp.float32
+    ).astype(jnp.bfloat16)
+    weighted = jnp.sum(weights_here * expert_out.astype(jnp.float32), axis=0).astype(jnp.bfloat16)
+    mixture = lax.psum_scatter(weighted, "expert", scatter_dimension=0, tiled=True)
+    residual = (mixture.astype(jnp.float32) - judge_output.astype(jnp.float32)).astype(jnp.bfloat16)
+    residual_rows = lax.all_gather(residual, "expert", axis=0, tiled=True).astype(jnp.float32)
+    inner = jnp.sum(expert_out.astype(jnp.float32) * residual_rows[None], axis=2)
+    inner_back = lax.all_to_all(
+        inner.reshape(exp_local, senders, tok_count).transpose(1, 0, 2),
+        "expert",
+        split_axis=0,
+        concat_axis=0,
+        tiled=True,
+    ).reshape(experts, tok_count)
+    route_grads = jnp.sum(jnp.where(chosen, inner_back.T[:, None, :], 0.0), axis=2)
+    out_grad = (weights_here * residual_rows[None]).astype(jnp.bfloat16)
+    hidden_grad = jnp.einsum("esd,efd->esf", out_grad, down_full, preferred_element_type=jnp.float32)
+    gate_grad = (hidden_grad * up_pre * sig_gate * (1.0 + gate_pre * (1.0 - sig_gate))).astype(
+        jnp.bfloat16
+    )
+    up_grad = (hidden_grad * gate_pre * sig_gate).astype(jnp.bfloat16)
+    parts = (
+        jnp.einsum("esf,sd->efd", gate_grad, rows, preferred_element_type=jnp.float32),
+        jnp.einsum("esf,sd->efd", up_grad, rows, preferred_element_type=jnp.float32),
+        jnp.einsum("esf,esd->efd", hidden, out_grad, preferred_element_type=jnp.float32),
+    )
+    grads = [
+        lax.psum_scatter(part.astype(jnp.bfloat16), "dp", scatter_dimension=1, tiled=True)
+        for part in parts
+    ]
+    return (mixture, route_grads, *grads)
+
+
+def on_device(student_input, judge_output, expert_ids, route_weights, w_gate, w_up, w_down):
+    experts = w_gate.shape[0] * lax.axis_size("expert")
+    form = dense_rows if experts <= 4 * expert_ids.shape[1] else routed_rows
+    return form(student_input, judge_output, expert_ids, route_weights, w_gate, w_up, w_down)
+
+
 def solution(mesh):
     placed = (
         P(("groups", "dp", "expert"), None),

time: 292 us -> 243 us (0.83)
  the two profiles are of different devices: /device:TPU:11 before, /device:TPU:0 now
where the time goes in v1:
time: 243 us
  waiting for transfers between devices  171 us (70%)
  matrix products  28.1 us (12%)
  between operations  13.8 us (6%)
  starting transfers between devices  11.1 us (5%)
  local copies, waits for them, and re-layouts  10.5 us (4%)
  other arithmetic  8.51 us (4%)
    unnamed x4, waiting for transfers between devices  70.6 us
    all_gather x1, waiting for transfers between devices, dense_rows(): lax.all_gather(residual, 'expert', axis=0, tiled=True).astype(jnp.float32)  53.4 us
    all_gather x1, waiting for transfers between devices, dense_rows(): rows = lax.all_gather(student_input, 'expert', axis=0, tiled=True)  46.8 us
    unnamed x21, local copies, waits for them, and re-layouts  10.5 us
    all_to_all x1, starting transfers between devices, dense_rows(): lax.all_to_all(dense_weights.T.reshape(senders, exp_local, tok_count), 'e...  7.36 us
    reduce_sum x1, other arithmetic, dense_rows(): jnp.sum(expert_out.astype(jnp.float32) * residual_rows[None], axis=2)  5.81 us
    dot_general x1, matrix products, dense_rows(): jnp.einsum('esf,efd->esd', hidden, down_full, preferred_element_type=jnp....  5.66 us
    dot_general x1, matrix products, dense_rows(): jnp.einsum('sd,efd->esf', rows, up_full, preferred_element_type=jnp.float32)  4.91 us
  transfers between devices with their start and end apart: 5, of which 3 were waited for; matrix products, arithmetic and copies ran while one was open for 10% of the time, Pallas kernels for 0%

profile of v1, /device:TPU:0, one launch (start us, length us, event | category | flops | bytes accessed | tf_op | source)
XLA Modules:
  0.0 242.9 jit_solution(8068700410483785708)
XLA Ops:
  7.2 0.0 copy-start
  7.2 0.0 all-gather.3.cloned.1.call-start
  7.2 0.7 all-gather.3.cloned.1.call-update
  7.9 1.3 select_reduce_fusion.1
  9.2 7.4 %all-to-all-start = ((f32[16,1,128]{2,1,0:T(1,128)}), f32[16,1,128]{2,1,0:T(1,128)S(1)}, u32[]{:S(2)}, u32[]{:S(2)}) async-start(f32[16,1,128]{2,1,0:T(1,128)} %bitcast.2), calls=%async_computation | async-start | bytes 16384 | tf_op jit(solution)/shard_map/all_to_all | solution.py:126
  16.6 0.0 reduce-scatter.4.cloned.1.call-start
  16.6 46.8 %all-gather.3.cloned.1.call-done = bf16[2048,1024]{1,0:T(8,128)(2,1)} async-done(((bf16[128,1024]{1,0:T(8,128)(2,1)}), bf16[2048,1024]{1,0:T(8,128)(2,1)}) %all-gather.3.cloned.1.call-update) | async-done | bytes 4194320 | tf_op jit(solution)/shard_map/all_gather | solution.py:125
  63.5 0.0 copy-start.4
  63.5 4.4 %fusion.51 = f32[384,2048]{1,0:T(8,128)S(1)} fusion(bf16[2048,1024]{1,0:T(8,128)(2,1)} %all-gather.3.cloned.1.call-done, bf16[1,384,1024]{2,1,0:T(8,128)(2,1)} %param.11), kind=kOutput, calls=%fused_computation.41 | convolution fusion | flops 1610612736 | bytes 8126464 | tf_op jit(solution)/shard_map/sd,efd->esf/dot_general | solution.py:134
  67.9 0.0 copy-start.6
  67.9 1.7 copy-done.6
  69.6 0.0 copy-done.4
  69.6 4.9 %fusion.7 = (bf16[1,2048,384]{1,2,0:T(8,128)(2,1)S(1)}, f32[384,2048]{1,0:T(8,128)}) fusion(f32[384,2048]{1,0:T(8,128)S(1)} %fusion.51, bf16[2048,1024]{1,0:T(8,128)(2,1)S(1)} %copy-done.4, bf16[1,384,1024]{2,1,0:T(8,128)(2,1)} %param.12), kind=kOutput, calls=%fused_computation.11 | convolution fusion | flops 1615331328 | bytes 12845056 | tf_op jit(solution)/shard_map/sd,efd->esf/dot_general | solution.py:135
  74.5 0.0 all-to-all-done
  74.5 0.0 copy-done
  74.5 5.7 %fusion = (bf16[2048,1024]{0,1:T(8,128)(2,1)}, bf16[2048,1024]{0,1:T(8,128)(2,1)}) fusion(f32[2048]{0:T(1024)S(1)} %bitcast.143, bf16[1,384,1024]{2,1,0:T(8,128)(2,1)S(1)} %copy-done, bf16[1,2048,384]{1,2,0:T(8,128)(2,1)S(1)} %get-tuple-element.25), kind=kOutput, calls=%fused_computation.3 | convolution fusion | flops 1619001344 | bytes 10756096 | tf_op jit(solution)/shard_map/esf,efd->esd/dot_general | solution.py:138
  80.1 6.4 %copy.36 = bf16[2048,1024]{1,0:T(8,128)(2,1)} copy(bf16[2048,1024]{0,1:T(8,128)(2,1)} %get-tuple-element.27) | data formatting | bytes 8388608
  86.5 0.0 copy-start.2
  86.5 0.0 reduce-scatter.4.cloned.1.call-update
  86.5 0.0 all-gather.5.cloned.1.call-start
  86.6 0.9 copy-done.2
  87.5 0.2 copy.31
  87.6 69.9 %reduce-scatter.4.cloned.1.call-done = bf16[128,1024]{1,0:T(8,128)(2,1)} async-done(((bf16[2048,1024]{1,0:T(8,128)(2,1)}), bf16[128,1024]{1,0:T(8,128)(2,1)}) %reduce-scatter.4.cloned.1.call-update) | async-done | bytes 262160
  157.5 1.1 copy.37
  158.7 0.8 subtract_convert_fusion
  159.4 0.0 all-gather.5.cloned.1.call-update
  159.5 53.4 %all-gather.5.cloned.1.call-done = bf16[2048,1024]{0,1:T(8,128)(2,1)} async-done(((bf16[128,1024]{0,1:T(8,128)(2,1)}), bf16[2048,1024]{0,1:T(8,128)(2,1)}) %all-gather.5.cloned.1.call-update) | async-done | bytes 4194320 | tf_op jit(solution)/shard_map/all_gather | solution.py:144
  212.9 5.8 %fusion.1 = f32[2048]{0:T(1024)} fusion(bf16[2048,1024]{0,1:T(8,128)(2,1)} %all-gather.5.cloned.1.call-done, bf16[2048,1024]{0,1:T(8,128)(2,1)} %get-tuple-element.28), kind=kLoop, calls=%fused_computation.4 | loop fusion | flops 8386560 | bytes 8396800 | tf_op jit(solution)/shard_map/reduce_sum | solution.py:145
  218.7 3.6 %all-to-all-start.1 = ((f32[16,1,128]{2,1,0:T(1,128)}), f32[16,1,128]{2,1,0:T(1,128)S(1)}, u32[]{:S(2)}, u32[]{:S(2)}) async-start(f32[16,1,128]{2,1,0:T(1,128)} %bitcast.14), calls=%async_computation.1 | async-start | bytes 16384 | tf_op jit(solution)/shard_map/all_to_all | solution.py:146
  222.3 0.0 copy-start.5
  222.3 0.0 copy-start.7
  222.3 4.1 %fusion.5 = f32[2048,384]{0,1:T(8,128)S(1)} fusion(bf16[2048,1024]{0,1:T(8,128)(2,1)} %all-gather.5.cloned.1.call-done, f32[2048]{0:T(1024)S(1)} %bitcast.144, bf16[1,384,1024]{2,1,0:T(8,128)(2,1)S(1)} %copy-done), kind=kOutput, calls=%fused_computation.8 | convolution fusion | flops 1616904192 | bytes 8134656 | tf_op jit(solution)/shard_map/esd,efd->esf/dot_general | solution.py:155
  226.5 0.0 copy-done.5
  226.5 0.3 copy-done.7
  226.8 0.0 copy-start.8
  226.8 2.7 %fusion.41 = bf16[1,384,1024]{2,1,0:T(8,128)(2,1)} fusion(bf16[2048,1024]{1,0:T(8,128)(2,1)S(1)} %copy-done.5, f32[384,2048]{1,0:T(8,128)S(1)} %copy-done.7, f32[2048,384]{0,1:T(8,128)S(1)} %fusion.5), kind=kOutput, calls=%fused_computation.35 | convolution fusion | flops 1615724544 | bytes 11272192 | tf_op jit(solution)/shard_map/esf,sd->efd/dot_general | solution.py:162
  229.5 0.0 copy-done.8
  229.5 0.0 copy-start.1
  229.5 3.6 %fusion.44 = bf16[1,384,1024]{2,1,0:T(8,128)(2,1)} fusion(bf16[2048,1024]{1,0:T(8,128)(2,1)S(1)} %copy-done.5, f32[384,2048]{1,0:T(8,128)S(1)} %copy-done.7, f32[384,2048]{1,0:T(8,128)S(1)} %copy-done.8, f32[2048,384]{0,1:T(8,128)S(1)} %fusion.5), kind=kOutput, calls=%fused_computation.36 | convolution fusion | flops 1618870272 | bytes 14417920 | tf_op jit(solution)/shard_map/esf,sd->efd/dot_general | solution.py:161
  233.1 0.0 copy-done.1
  233.1 0.0 copy-start.3
  233.1 2.7 %fusion.36 = bf16[1,384,1024]{2,1,0:T(8,128)(2,1)} fusion(bf16[2048,1024]{0,1:T(8,128)(2,1)S(1)} %copy-done.1, f32[2048]{0:T(1024)S(1)} %bitcast.145, bf16[1,2048,384]{1,2,0:T(8,128)(2,1)S(1)} %get-tuple-element.25), kind=kOutput, calls=%fused_computation.34 | convolution fusion | flops 1617297408 | bytes 6561792 | tf_op jit(solution)/shard_map/esf,esd->efd/dot_general | solution.py:163
  235.8 0.0 all-to-all-done.1
  235.8 0.0 copy-done.3
  235.8 0.6 select_reduce_fusion
Async XLA Ops:
  7.2 67.3 %copy-start = (bf16[1,384,1024]{2,1,0:T(8,128)(2,1)S(1)}, bf16[1,384,1024]{2,1,0:T(8,128)(2,1)}, u32[]{:S(2)}) copy-start(bf16[1,384,1024]{2,1,0:T(8,128)(2,1)} %param.13) | copy-start | bytes 2359300
  7.2 56.3 %all-gather.3.cloned.1.call-start = ((), (), s32[]{:S(2)}) async-start(), calls=%async_computation.3 | async-start | bytes 4456448 | tf_op jit(solution)/shard_map/all_gather | solution.py:125
  9.2 65.2 %all-to-all-start = ((f32[16,1,128]{2,1,0:T(1,128)}), f32[16,1,128]{2,1,0:T(1,128)S(1)}, u32[]{:S(2)}, u32[]{:S(2)}) async-start(f32[16,1,128]{2,1,0:T(1,128)} %bitcast.2), calls=%async_computation | async-start | bytes 16384 | tf_op jit(solution)/shard_map/all_to_all | solution.py:126
  16.6 140.9 %reduce-scatter.4.cloned.1.call-start = ((), (), s32[]{:S(2)}) async-start(), calls=%async_computation.5 | async-start | bytes 4456448
  63.5 6.1 %copy-start.4 = (bf16[2048,1024]{1,0:T(8,128)(2,1)S(1)}, bf16[2048,1024]{1,0:T(8,128)(2,1)}, u32[]{:S(2)}) copy-start(bf16[2048,1024]{1,0:T(8,128)(2,1)} %all-gather.3.cloned.1.call-done) | copy-start | bytes 12582916
  67.9 1.7 copy-start.6
  86.5 0.9 copy-start.2
  86.5 126.4 %all-gather.5.cloned.1.call-start = ((), (), s32[]{:S(2)}) async-start(), calls=%async_computation.4 | async-start | bytes 4456448 | tf_op jit(solution)/shard_map/all_gather | solution.py:144
  218.7 17.1 %all-to-all-start.1 = ((f32[16,1,128]{2,1,0:T(1,128)}), f32[16,1,128]{2,1,0:T(1,128)S(1)}, u32[]{:S(2)}, u32[]{:S(2)}) async-start(f32[16,1,128]{2,1,0:T(1,128)} %bitcast.14), calls=%async_computation.1 | async-start | bytes 16384 | tf_op jit(solution)/shard_map/all_to_all | solution.py:146
  222.3 4.2 %copy-start.5 = (bf16[2048,1024]{1,0:T(8,128)(2,1)S(1)}, bf16[2048,1024]{1,0:T(8,128)(2,1)}, u32[]{:S(2)}) copy-start(bf16[2048,1024]{1,0:T(8,128)(2,1)} %all-gather.3.cloned.1.call-done) | copy-start | bytes 12582916
  222.3 4.4 %copy-start.7 = (f32[384,2048]{1,0:T(8,128)S(1)}, f32[384,2048]{1,0:T(8,128)}, u32[]{:S(2)}) copy-start(f32[384,2048]{1,0:T(8,128)} %copy-done.6) | copy-start | bytes 9437188
  226.8 2.7 %copy-start.8 = (f32[384,2048]{1,0:T(8,128)S(1)}, f32[384,2048]{1,0:T(8,128)}, u32[]{:S(2)}) copy-start(f32[384,2048]{1,0:T(8,128)} %get-tuple-element.26) | copy-start | bytes 9437188
  229.5 3.6 %copy-start.1 = (bf16[2048,1024]{0,1:T(8,128)(2,1)S(1)}, bf16[2048,1024]{0,1:T(8,128)(2,1)}, u32[]{:S(2)}) copy-start(bf16[2048,1024]{0,1:T(8,128)(2,1)} %all-gather.5.cloned.1.call-done) | copy-start | bytes 12582916
  233.1 2.7 %copy-start.3 = (s32[128,8]{0,1:T(8,128)S(1)}, s32[128,8]{0,1:T(8,128)}, u32[]{:S(2)}) copy-start(s32[128,8]{0,1:T(8,128)} %param.9) | copy-start | bytes 12292
Sparse Core Ops, SparseCore 0:
  10.2 53.2 all-gather.2
  86.6 70.8 reduce-scatter.3
  160.5 52.3 all-gather.4

commit v2 on v1

--- a/solution.py
+++ b/solution.py
@@ -1,8 +1,11 @@
+import functools
 import math
 
 import jax
 import jax.numpy as jnp
 from jax import lax
+from jax.experimental import pallas as pl
+from jax.experimental.pallas import tpu as pltpu
 from jax.sharding import PartitionSpec as P
 
 
@@ -110,6 +113,335 @@
     )
 
 
+UP, DOWN, ACROSS, SIBLING = range(4)
+MESH = pl.DeviceIdType.MESH
+
+
+def place(senders):
+    me = lax.axis_index("expert")
+    depth = senders // 4
+    z, x, c = me // 4, (me // 2) % 2, me % 2
+    return depth, z, x, c
+
+
+def index_of(z, x, c):
+    return z * 4 + x * 2 + c
+
+
+def remote(src, dst, send_sem, recv_sem, device):
+    return pltpu.make_async_remote_copy(
+        src_ref=src,
+        dst_ref=dst,
+        send_sem=send_sem,
+        recv_sem=recv_sem,
+        device_id={"expert": device},
+        device_id_type=MESH,
+    )
+
+
+def greet_all(senders):
+    me = lax.axis_index("expert")
+    barrier = pltpu.get_barrier_semaphore()
+    for step in range(1, senders):
+        other = lax.rem(me + step, senders)
+        pl.semaphore_signal(barrier, inc=1, device_id={"expert": other}, device_id_type=MESH)
+    pl.semaphore_wait(barrier, senders - 1)
+
+
+def gather_blocks(senders, out, send_sem, recv_sem):
+    depth, z, x, c = place(senders)
+    targets = {
+        UP: lambda: index_of(z + 1, x, c),
+        DOWN: lambda: index_of(z - 1, x, c),
+        ACROSS: lambda: index_of(z, 1 - x, c),
+        SIBLING: lambda: index_of(z, x, 1 - c),
+    }
+
+    def copy(slot, way):
+        return remote(
+            out.at[slot], out.at[slot], send_sem.at[slot, way], recv_sem.at[slot], targets[way]()
+        )
+
+    def each_column_copy(act):
+        own = index_of(z, x, c)
+        pl.when(z < depth - 1)(lambda: act(own, UP, None))
+        pl.when(z > 0)(lambda: act(own, DOWN, None))
+        act(own, ACROSS, None)
+        act(own, SIBLING, None)
+        for d in range(1, depth):
+            from_below, from_above = index_of(z - d, x, c), index_of(z + d, x, c)
+
+            @pl.when(z - d >= 0)
+            def _():
+                act(None, None, from_below)
+                pl.when(z < depth - 1)(lambda: act(from_below, UP, None))
+                act(from_below, ACROSS, None)
+                act(from_below, SIBLING, None)
+
+            @pl.when(z + d < depth)
+            def _():
+                act(None, None, from_above)
+                pl.when(z > 0)(lambda: act(from_above, DOWN, None))
+                act(from_above, ACROSS, None)
+                act(from_above, SIBLING, None)
+
+    def arrive_or_start(slot, way, arrival):
+        if arrival is None:
+            copy(slot, way).start()
+        else:
+            copy(arrival, ACROSS).wait_recv()
+
+    def finish(slot, way, arrival):
+        if arrival is None:
+            copy(slot, way).wait_send()
+
+    def across_order():
+        yield z, None
+        for d in range(1, depth):
+            yield z - d, z - d >= 0
+            yield z + d, z + d < depth
+
+    each_column_copy(arrive_or_start)
+    for zb, here in across_order():
+
+        def pass_on(zb=zb):
+            slot = index_of(zb, 1 - x, c)
+            copy(slot, ACROSS).wait_recv()
+            copy(slot, SIBLING).start()
+
+        pass_on() if here is None else pl.when(here)(pass_on)
+    for zb in range(depth):
+        for xb in range(2):
+            copy(index_of(zb, xb, 1 - c), ACROSS).wait_recv()
+    each_column_copy(finish)
+    for zb in range(depth):
+        copy(index_of(zb, 1 - x, c), SIBLING).wait_send()
+
+
+def spread_kernel(
+    senders, row_ref, weight_ref, out, weight_out, send_sem, recv_sem, weight_send, weight_recv
+):
+    me = lax.axis_index("expert")
+    out[me] = row_ref[...]
+    weight_out[me] = weight_ref[me]
+    greet_all(senders)
+
+    def weight_copy(step):
+        other = lax.rem(me + step, senders)
+        return remote(
+            weight_ref.at[other],
+            weight_out.at[me],
+            weight_send.at[other],
+            weight_recv.at[me],
+            other,
+        )
+
+    def weight_arrival(step):
+        other = lax.rem(me + step, senders)
+        return remote(
+            weight_ref.at[other],
+            weight_out.at[other],
+            weight_send.at[other],
+            weight_recv.at[other],
+            other,
+        )
+
+    for step in range(1, senders):
+        weight_copy(step).start()
+    gather_blocks(senders, out, send_sem, recv_sem)
+    for step in range(1, senders):
+        weight_arrival(step).wait_recv()
+        weight_copy(step).wait_send()
+
+
+def mix_kernel(
+    senders,
+    part_ref,
+    judge_ref,
+    mixture_ref,
+    out,
+    sib_in,
+    x_out,
+    x_in,
+    z_out,
+    up_in,
+    down_in,
+    out_total,
+    sib_send,
+    sib_recv,
+    x_send,
+    x_recv,
+    z_send,
+    up_recv,
+    down_recv,
+    send_sem,
+    recv_sem,
+):
+    depth, z, x, c = place(senders)
+    greet_all(senders)
+
+    def by_distance(act):
+        for d in range(depth - 1, 0, -1):
+            pl.when(z + d < depth)(functools.partial(act, z + d, UP))
+            pl.when(z - d >= 0)(functools.partial(act, z - d, DOWN))
+        act(z, None)
+
+    def sib_copy(zb, xb):
+        slot = zb * 2 + xb
+        return remote(
+            part_ref.at[index_of(zb, xb, 1 - c)],
+            sib_in.at[slot],
+            sib_send.at[slot],
+            sib_recv.at[slot],
+            index_of(z, x, 1 - c),
+        )
+
+    def x_copy(zb):
+        return remote(
+            x_out.at[zb], x_in.at[zb], x_send.at[zb], x_recv.at[zb], index_of(z, 1 - x, c)
+        )
+
+    def up_copy(zb):
+        return remote(
+            z_out.at[zb], up_in.at[zb], z_send.at[zb], up_recv.at[zb], index_of(z + 1, x, c)
+        )
+
+    def down_copy(zb):
+        return remote(
+            z_out.at[zb], down_in.at[zb], z_send.at[zb], down_recv.at[zb], index_of(z - 1, x, c)
+        )
+
+    def start_sibling(zb, way):
+        sib_copy(zb, 1 - x).start()
+        sib_copy(zb, x).start()
+
+    def pair_sum(zb, xb):
+        sib_copy(zb, xb).wait_recv()
+        mine = part_ref[index_of(zb, xb, c)].astype(jnp.float32)
+        return mine + sib_in[zb * 2 + xb].astype(jnp.float32)
+
+    def send_across(zb, way):
+        x_out[zb] = pair_sum(zb, 1 - x).astype(jnp.bfloat16)
+        x_copy(zb).start()
+
+    def chip_sum(zb):
+        total = pair_sum(zb, x)
+        x_copy(zb).wait_recv()
+        return total + x_in[zb].astype(jnp.float32)
+
+    def send_along(zb, way):
+        total = chip_sum(zb)
+        if way is None:
+            out_total[...] = total
+
+            @pl.when(z > 0)
+            def _():
+                up_copy(zb).wait_recv()
+                out_total[...] += up_in[zb].astype(jnp.float32)
+
+            @pl.when(z < depth - 1)
+            def _():
+                down_copy(zb).wait_recv()
+                out_total[...] += down_in[zb].astype(jnp.float32)
+
+            return
+        z_out[zb] = total.astype(jnp.bfloat16)
+        step_copy, landed, here = (
+            (up_copy, up_in, z > 0) if way == UP else (down_copy, down_in, z < depth - 1)
+        )
+
+        @pl.when(here)
+        def _():
+            step_copy(zb).wait_recv()
+            more = pair_again(zb) + landed[zb].astype(jnp.float32)
+            z_out[zb] = more.astype(jnp.bfloat16)
+
+        step_copy(zb).start()
+
+    def pair_again(zb):
+        mine = part_ref[index_of(zb, x, c)].astype(jnp.float32)
+        return mine + sib_in[zb * 2 + x].astype(jnp.float32) + x_in[zb].astype(jnp.float32)
+
+    def finish(zb, way):
+        sib_copy(zb, 1 - x).wait_send()
+        sib_copy(zb, x).wait_send()
+        x_copy(zb).wait_send()
+        if way is not None:
+            (up_copy if way == UP else down_copy)(zb).wait_send()
+
+    by_distance(start_sibling)
+    by_distance(send_across)
+    by_distance(send_along)
+    mixture = out_total[...]
+    mixture_ref[...] = mixture.astype(jnp.bfloat16)
+    out[index_of(z, x, c)] = (mixture - judge_ref[...].astype(jnp.float32)).astype(jnp.bfloat16)
+    gather_blocks(senders, out, send_sem, recv_sem)
+    by_distance(finish)
+
+
+def vmem_specs(count):
+    return [pl.BlockSpec(memory_space=pltpu.VMEM)] * count
+
+
+def spread_rows(rows, weights):
+    senders = weights.shape[0]
+    dma = pltpu.SemaphoreType.DMA
+    return pl.pallas_call(
+        functools.partial(spread_kernel, senders),
+        out_shape=(
+            jax.ShapeDtypeStruct((senders, *rows.shape), rows.dtype),
+            jax.ShapeDtypeStruct(weights.shape, weights.dtype),
+        ),
+        in_specs=vmem_specs(2),
+        out_specs=tuple(vmem_specs(2)),
+        scratch_shapes=[dma((senders, 4)), dma((senders,)), dma((senders,)), dma((senders,))],
+        compiler_params=pltpu.CompilerParams(
+            collective_id=0, has_side_effects=True, vmem_limit_bytes=16 << 20
+        ),
+    )(rows, weights)
+
+
+def mix_rows(parts, judge):
+    senders = parts.shape[0]
+    depth = senders // 4
+    block = judge.shape
+    dma = pltpu.SemaphoreType.DMA
+
+    def blocks(count):
+        return pltpu.VMEM((count, *block), jnp.bfloat16)
+
+    return pl.pallas_call(
+        functools.partial(mix_kernel, senders),
+        out_shape=(
+            jax.ShapeDtypeStruct(block, jnp.bfloat16),
+            jax.ShapeDtypeStruct((senders, *block), jnp.bfloat16),
+        ),
+        in_specs=vmem_specs(2),
+        out_specs=tuple(vmem_specs(2)),
+        scratch_shapes=[
+            blocks(2 * depth),
+            blocks(depth),
+            blocks(depth),
+            blocks(depth),
+            blocks(depth),
+            blocks(depth),
+            pltpu.VMEM(block, jnp.float32),
+            dma((2 * depth,)),
+            dma((2 * depth,)),
+            dma((depth,)),
+            dma((depth,)),
+            dma((depth,)),
+            dma((depth,)),
+            dma((depth,)),
+            dma((senders, 4)),
+            dma((senders,)),
+        ],
+        compiler_params=pltpu.CompilerParams(
+            collective_id=1, has_side_effects=True, vmem_limit_bytes=32 << 20
+        ),
+    )(parts, judge)
+
+
 def dense_rows(student_input, judge_output, expert_ids, route_weights, w_gate, w_up, w_down):
     senders = lax.axis_size("expert")
     exp_local = w_gate.shape[0]
@@ -122,15 +454,12 @@
     )
     chosen = expert_ids[:, :, None] == jnp.arange(experts, dtype=jnp.int32)[None, None, :]
     dense_weights = jnp.sum(jnp.where(chosen, route_weights[:, :, None], 0.0), axis=1)
-    rows = lax.all_gather(student_input, "expert", axis=0, tiled=True)
-    weights_here = lax.all_to_all(
-        dense_weights.T.reshape(senders, exp_local, tok_count),
-        "expert",
-        split_axis=0,
-        concat_axis=0,
-        tiled=True,
-    )
-    weights_here = weights_here.transpose(1, 0, 2).reshape(exp_local, senders * tok_count, 1)
+    by_expert = dense_weights.T.reshape(senders, exp_local, tok_count)
+    padded = jnp.pad(by_expert, ((0, 0), (0, -exp_local % 8), (0, 0)))
+    rows, weights_here = spread_rows(student_input, padded)
+    rows = rows.reshape(senders * tok_count, dim_model)
+    weights_here = weights_here[:, :exp_local].transpose(1, 0, 2)
+    weights_here = weights_here.reshape(exp_local, senders * tok_count, 1)
     gate_pre = jnp.einsum("sd,efd->esf", rows, gate_full, preferred_element_type=jnp.float32)
     up_pre = jnp.einsum("sd,efd->esf", rows, up_full, preferred_element_type=jnp.float32)
     sig_gate = jax.nn.sigmoid(gate_pre)
@@ -139,9 +468,8 @@
         "esf,efd->esd", hidden, down_full, preferred_element_type=jnp.float32
     ).astype(jnp.bfloat16)
     weighted = jnp.sum(weights_here * expert_out.astype(jnp.float32), axis=0).astype(jnp.bfloat16)
-    mixture = lax.psum_scatter(weighted, "expert", scatter_dimension=0, tiled=True)
-    residual = (mixture.astype(jnp.float32) - judge_output.astype(jnp.float32)).astype(jnp.bfloat16)
-    residual_rows = lax.all_gather(residual, "expert", axis=0, tiled=True).astype(jnp.float32)
+    mixture, residual_rows = mix_rows(weighted.reshape(senders, tok_count, dim_model), judge_output)
+    residual_rows = residual_rows.reshape(senders * tok_count, dim_model).astype(jnp.float32)
     inner = jnp.sum(expert_out.astype(jnp.float32) * residual_rows[None], axis=2)
     inner_back = lax.all_to_all(
         inner.reshape(exp_local, senders, tok_count).transpose(1, 0, 2),
@@ -171,7 +499,8 @@
 
 def on_device(student_input, judge_output, expert_ids, route_weights, w_gate, w_up, w_down):
     experts = w_gate.shape[0] * lax.axis_size("expert")
-    form = dense_rows if experts <= 4 * expert_ids.shape[1] else routed_rows
+    dense = experts <= 4 * expert_ids.shape[1] and lax.axis_size("expert") % 4 == 0
+    form = dense_rows if dense else routed_rows
     return form(student_input, judge_output, expert_ids, route_weights, w_gate, w_up, w_down)
 
 

time: 243 us -> 129 us (0.53)
  waiting for transfers between devices: 171 us -> 0.01 us
  Pallas kernels: 0 us -> 94.7 us
  between operations: 13.8 us -> 0.81 us
  local copies, waits for them, and re-layouts: 10.5 us -> 1.71 us
  starting transfers between devices: 11.1 us -> 4.08 us
  other arithmetic: 8.51 us -> 3.37 us
  matrix products: 28.1 us -> 24.2 us
    all_gather x2 -> x0, waiting for transfers between devices: 100 us -> none  [the longest x1 53.4 us: dense_rows(): lax.all_gather(residual, 'expert', axis=0, tiled=True).astype(jnp.float32)]
    pallas_call x0 -> x2, Pallas kernels: none -> 94.7 us  [the longest x1 58.7 us: mix_rows(): pl.pallas_call(functools.partial(mix_kernel, senders), out_shape=(jax.Sha...]
    unnamed x4 -> x0, waiting for transfers between devices: 70.6 us -> none
    unnamed x21 -> x25, local copies, waits for them, and re-layouts: 10.5 us -> 1.7 us
    all_to_all x1 -> x0, starting transfers between devices: 7.36 us -> none  [dense_rows(): lax.all_to_all(dense_weights.T.reshape(senders, exp_local, tok_count), 'e...]
    reduce_sum x1, other arithmetic: 5.81 us -> 1.97 us  [dense_rows(): jnp.sum(expert_out.astype(jnp.float32) * residual_rows[None], axis=2)]
    dot_general x1, matrix products: 5.66 us -> 2.35 us  [dense_rows(): jnp.einsum('esf,efd->esd', hidden, down_full, preferred_element_type=jnp....]
  transfers between devices with their start and end apart: 5 -> 1, of which waited for: 3 -> 0; matrix products, arithmetic and copies ran while one was open for 10% -> 10% of each run, Pallas kernels for 0% -> 0%
where the time goes in v2:
time: 129 us
  Pallas kernels  94.7 us (73%)
  matrix products  24.2 us (19%)
  starting transfers between devices  4.08 us (3%)
  other arithmetic  3.37 us (3%)
  local copies, waits for them, and re-layouts  1.71 us (1%)
    pallas_call x1, Pallas kernels, mix_rows(): pl.pallas_call(functools.partial(mix_kernel, senders), out_shape=(jax.Sha...  58.7 us
    pallas_call x1, Pallas kernels, spread_rows(): pl.pallas_call(functools.partial(spread_kernel, senders), out_shape=(jax....  36 us
    dot_general x1, matrix products, dense_rows(): jnp.einsum('esd,efd->esf', out_grad, down_full, preferred_element_type=jn...  4.72 us
    dot_general x1, matrix products, dense_rows(): jnp.einsum('sd,efd->esf', rows, up_full, preferred_element_type=jnp.float32)  4.54 us
    dot_general x1, matrix products, dense_rows(): jnp.einsum('sd,efd->esf', rows, gate_full, preferred_element_type=jnp.flo...  4.18 us
    all_to_all x1, starting transfers between devices, dense_rows(): lax.all_to_all(inner.reshape(exp_local, senders, tok_count).transpose(1,...  4.08 us
    dot_general x1, matrix products, dense_rows(): jnp.einsum('esf,sd->efd', gate_grad, rows, preferred_element_type=jnp.flo...  2.91 us
    dot_general x1, matrix products, dense_rows(): jnp.einsum('esf,esd->efd', hidden, out_grad, preferred_element_type=jnp.f...  2.79 us
  transfers between devices with their start and end apart: 1, of which 0 were waited for; matrix products, arithmetic and copies ran while one was open for 10% of the time, Pallas kernels for 0%

profile of v2, /device:TPU:0, one launch (start us, length us, event | category | flops | bytes accessed | tf_op | source)
XLA Modules:
  0.0 128.9 jit_solution(7526158208309652399)
XLA Ops:
  0.6 0.0 copy-start
  0.6 0.8 select_reduce_fusion.1
  1.5 0.0 copy-start.4
  1.5 0.9 copy-done.4
  2.4 36.0 %shard_map.110 = (bf16[16,128,1024]{2,1,0:T(8,128)(2,1)S(1)}, f32[16,8,128]{2,1,0:T(8,128)S(1)}) custom-call(bf16[128,1024]{1,0:T(8,128)(2,1)S(1)} %copy-done.4, f32[16,8,128]{2,1,0:T(8,128)S(1)} %pad.4.weight_ref), custom_call_target="tpu_custom_call" | custom-call | tf_op jit(solution)/shard_map/pallas_call | solution.py:389
  38.4 0.0 copy-start.5
  38.4 0.0 copy-start.8
  38.4 4.2 %fusion.45 = f32[2048,384]{1,0:T(8,128)S(1)} fusion(bf16[2048,1024]{1,0:T(8,128)(2,1)S(1)} %bitcast.157, bf16[1,384,1024]{2,1,0:T(8,128)(2,1)} %param.11), kind=kOutput, calls=%fused_computation.41 | convolution fusion | flops 1610612736 | bytes 8126464 | tf_op jit(solution)/shard_map/sd,efd->esf/dot_general | solution.py:463
  42.6 0.0 copy-done.5
  42.6 0.0 copy-done.8
  42.6 0.0 copy-start.9
  42.7 4.5 %fusion.3 = (bf16[1,2048,384]{2,1,0:T(8,128)(2,1)S(1)}, f32[2048,384]{1,0:T(8,128)}) fusion(f32[2048,384]{1,0:T(8,128)S(1)} %fusion.45, bf16[2048,1024]{1,0:T(8,128)(2,1)S(1)} %bitcast.158, bf16[1,384,1024]{2,1,0:T(8,128)(2,1)S(1)} %copy-done.8), kind=kOutput, calls=%fused_computation.9 | convolution fusion | flops 1615331328 | bytes 12845056 | tf_op jit(solution)/shard_map/sd,efd->esf/dot_general | solution.py:464
  47.2 0.0 copy-done.9
  47.2 0.0 copy-done
  47.2 0.0 copy-start.3
  47.2 2.3 %fusion = (bf16[2048,1024]{1,0:T(8,128)(2,1)S(1)}, bf16[2048,1024]{1,0:T(8,128)(2,1)S(1)}) fusion(f32[2048]{0:T(1024)S(1)} %bitcast.161, bf16[1,384,1024]{2,1,0:T(8,128)(2,1)S(1)} %copy-done, bf16[1,2048,384]{2,1,0:T(8,128)(2,1)S(1)} %get-tuple-element.13), kind=kOutput, calls=%fused_computation.2 | convolution fusion | flops 1619001344 | bytes 10756096 | tf_op jit(solution)/shard_map/esf,efd->esd/dot_general | solution.py:467
  49.6 0.0 copy-done.3
  49.6 58.7 %shard_map.111 = (bf16[128,1024]{1,0:T(8,128)(2,1)S(1)}, bf16[16,128,1024]{2,1,0:T(8,128)(2,1)S(1)}) custom-call(bf16[16,128,1024]{2,1,0:T(8,128)(2,1)S(1)} %bitcast.154, bf16[128,1024]{1,0:T(8,128)(2,1)S(1)} %copy-done.3), custom_call_target="tpu_custom_call" | custom-call | tf_op jit(solution)/shard_map/pallas_call | solution.py:413
  108.3 0.0 copy-start.1
  108.3 2.0 %fusion.1 = f32[2048]{0:T(1024)} fusion(bf16[2048,1024]{1,0:T(8,128)(2,1)S(1)} %get-tuple-element.16, bf16[16,128,1024]{2,1,0:T(8,128)(2,1)S(1)} %get-tuple-element.12), kind=kLoop, calls=%fused_computation.3 | loop fusion | flops 8386560 | bytes 8396800 | tf_op jit(solution)/shard_map/reduce_sum | solution.py:473
  110.2 0.0 copy-done.1
  110.3 4.1 %all-to-all-start = ((f32[16,1,128]{2,1,0:T(1,128)}), f32[16,1,128]{2,1,0:T(1,128)S(1)}, u32[]{:S(2)}, u32[]{:S(2)}) async-start(f32[16,1,128]{2,1,0:T(1,128)} %bitcast.19), calls=%async_computation | async-start | bytes 16384 | tf_op jit(solution)/shard_map/all_to_all | solution.py:474
  114.3 0.0 copy-start.6
  114.4 0.0 copy-start.10
  114.4 4.7 %fusion.40 = f32[2048,384]{1,0:T(8,128)S(1)} fusion(bf16[1,384,1024]{2,1,0:T(8,128)(2,1)S(1)} %copy-done, f32[2048]{0:T(1024)S(1)} %bitcast.162, bf16[1,2048,1,1,1,1,1024]{6,1,5,4,3,2,0:T(8,128)(2,1)} %bitcast.155), kind=kOutput, calls=%fused_computation.36 | convolution fusion | flops 1616904192 | bytes 8134656 | tf_op jit(solution)/shard_map/esd,efd->esf/dot_general | solution.py:483
  119.1 0.0 copy-done.6
  119.1 0.0 copy-done.10
  119.1 0.0 copy-start.11
  119.1 2.7 %fusion.31 = bf16[1,384,1024]{2,1,0:T(8,128)(2,1)} fusion(bf16[2048,1024]{1,0:T(8,128)(2,1)S(1)} %bitcast.159, f32[2048,384]{1,0:T(8,128)S(1)} %copy-done.10, f32[2048,384]{1,0:T(8,128)S(1)} %fusion.40), kind=kOutput, calls=%fused_computation.33 | convolution fusion | flops 1615724544 | bytes 11272192 | tf_op jit(solution)/shard_map/esf,sd->efd/dot_general | solution.py:490
  121.9 0.0 copy-done.11
  121.9 0.0 copy-start.2
  121.9 2.9 %fusion.34 = bf16[1,384,1024]{2,1,0:T(8,128)(2,1)} fusion(bf16[2048,1024]{1,0:T(8,128)(2,1)S(1)} %bitcast.160, f32[2048,384]{1,0:T(8,128)S(1)} %copy-done.10, f32[2048,384]{1,0:T(8,128)S(1)} %copy-done.11, f32[2048,384]{1,0:T(8,128)S(1)} %fusion.40), kind=kOutput, calls=%fused_computation.34 | convolution fusion | flops 1618870272 | bytes 14417920 | tf_op jit(solution)/shard_map/esf,sd->efd/dot_general | solution.py:489
  124.8 0.0 copy-done.2
  124.8 0.0 copy-start.7
  124.8 2.8 %fusion.37 = bf16[1,384,1024]{2,1,0:T(8,128)(2,1)} fusion(bf16[1,2048,384]{2,1,0:T(8,128)(2,1)S(1)} %get-tuple-element.13, f32[2048]{0:T(1024)S(1)} %bitcast.163, bf16[1,2048,1,1,1,1,1024]{6,1,5,4,3,2,0:T(8,128)(2,1)S(1)} %bitcast.156), kind=kOutput, calls=%fused_computation.35 | convolution fusion | flops 1617297408 | bytes 6561792 | tf_op jit(solution)/shard_map/esf,esd->efd/dot_general | solution.py:491
  127.6 0.0 all-to-all-done
  127.6 0.0 copy-done.7
  127.6 0.6 select_reduce_fusion
  128.2 0.7 copy.23
  (2 shorter events, 0.0 us)
Async XLA Ops:
  0.6 46.6 %copy-start = (bf16[1,384,1024]{2,1,0:T(8,128)(2,1)S(1)}, bf16[1,384,1024]{2,1,0:T(8,128)(2,1)}, u32[]{:S(2)}) copy-start(bf16[1,384,1024]{2,1,0:T(8,128)(2,1)} %param.13) | copy-start | bytes 2359300
  1.5 1.0 copy-start.4
  38.4 4.2 %copy-start.5 = (bf16[16,128,1024]{2,1,0:T(8,128)(2,1)}, bf16[16,128,1024]{2,1,0:T(8,128)(2,1)S(1)}, u32[]{:S(2)}) copy-start(bf16[16,128,1024]{2,1,0:T(8,128)(2,1)S(1)} %get-tuple-element.10) | copy-start | bytes 12582916
  38.4 4.2 %copy-start.8 = (bf16[1,384,1024]{2,1,0:T(8,128)(2,1)S(1)}, bf16[1,384,1024]{2,1,0:T(8,128)(2,1)}, u32[]{:S(2)}) copy-start(bf16[1,384,1024]{2,1,0:T(8,128)(2,1)} %param.12) | copy-start | bytes 2359300
  42.6 4.5 %copy-start.9 = (f32[2048,384]{1,0:T(8,128)}, f32[2048,384]{1,0:T(8,128)S(1)}, u32[]{:S(2)}) copy-start(f32[2048,384]{1,0:T(8,128)S(1)} %fusion.45) | copy-start | bytes 9437188
  47.2 2.4 %copy-start.3 = (bf16[128,1024]{1,0:T(8,128)(2,1)S(1)}, bf16[128,1024]{1,0:T(8,128)(2,1)}, u32[]{:S(2)}) copy-start(bf16[128,1024]{1,0:T(8,128)(2,1)} %judge_ref.1) | copy-start | bytes 786436
  108.3 2.0 %copy-start.1 = (bf16[16,128,1024]{2,1,0:T(8,128)(2,1)}, bf16[16,128,1024]{2,1,0:T(8,128)(2,1)S(1)}, u32[]{:S(2)}) copy-start(bf16[16,128,1024]{2,1,0:T(8,128)(2,1)S(1)} %get-tuple-element.12) | copy-start | bytes 12582916
  110.3 17.3 %all-to-all-start = ((f32[16,1,128]{2,1,0:T(1,128)}), f32[16,1,128]{2,1,0:T(1,128)S(1)}, u32[]{:S(2)}, u32[]{:S(2)}) async-start(f32[16,1,128]{2,1,0:T(1,128)} %bitcast.19), calls=%async_computation | async-start | bytes 16384 | tf_op jit(solution)/shard_map/all_to_all | solution.py:474
  114.3 4.8 %copy-start.6 = (bf16[16,128,1024]{2,1,0:T(8,128)(2,1)S(1)}, bf16[16,128,1024]{2,1,0:T(8,128)(2,1)}, u32[]{:S(2)}) copy-start(bf16[16,128,1024]{2,1,0:T(8,128)(2,1)} %copy-done.5) | copy-start | bytes 12582916
  114.4 4.8 %copy-start.10 = (f32[2048,384]{1,0:T(8,128)S(1)}, f32[2048,384]{1,0:T(8,128)}, u32[]{:S(2)}) copy-start(f32[2048,384]{1,0:T(8,128)} %copy-done.9) | copy-start | bytes 9437188
  119.1 2.8 %copy-start.11 = (f32[2048,384]{1,0:T(8,128)S(1)}, f32[2048,384]{1,0:T(8,128)}, u32[]{:S(2)}) copy-start(f32[2048,384]{1,0:T(8,128)} %get-tuple-element.14) | copy-start | bytes 9437188
  121.9 2.9 %copy-start.2 = (bf16[16,128,1024]{2,1,0:T(8,128)(2,1)S(1)}, bf16[16,128,1024]{2,1,0:T(8,128)(2,1)}, u32[]{:S(2)}) copy-start(bf16[16,128,1024]{2,1,0:T(8,128)(2,1)} %copy-done.1) | copy-start | bytes 12582916
  124.8 2.8 %copy-start.7 = (s32[128,8]{0,1:T(8,128)S(1)}, s32[128,8]{0,1:T(8,128)}, u32[]{:S(2)}) copy-start(s32[128,8]{0,1:T(8,128)} %param.9) | copy-start | bytes 12292

commit v3 on v0

--- a/solution.py
+++ b/solution.py
@@ -1,8 +1,11 @@
+import functools
 import math
 
 import jax
 import jax.numpy as jnp
 from jax import lax
+from jax.experimental import pallas as pl
+from jax.experimental.pallas import tpu as pltpu
 from jax.sharding import PartitionSpec as P
 
 
@@ -37,7 +40,7 @@
     return (gate_pre, up_pre, hidden)
 
 
-def on_device(student_input, judge_output, expert_ids, route_weights, w_gate, w_up, w_down):
+def routed_rows(student_input, judge_output, expert_ids, route_weights, w_gate, w_up, w_down):
     tok_count, dim_model = student_input.shape
     top_picks = expert_ids.shape[1]
     exp_local = w_gate.shape[0]
@@ -110,6 +113,428 @@
     )
 
 
+UP, DOWN, ACROSS, SIBLING = range(4)
+MESH = pl.DeviceIdType.MESH
+
+
+def place(senders):
+    me = lax.axis_index("expert")
+    depth = senders // 4
+    z, x, c = me // 4, (me // 2) % 2, me % 2
+    return depth, z, x, c
+
+
+def index_of(z, x, c):
+    return z * 4 + x * 2 + c
+
+
+def remote(src, dst, send_sem, recv_sem, device):
+    return pltpu.make_async_remote_copy(
+        src_ref=src,
+        dst_ref=dst,
+        send_sem=send_sem,
+        recv_sem=recv_sem,
+        device_id={"expert": device},
+        device_id_type=MESH,
+    )
+
+
+def greet_all(senders):
+    me = lax.axis_index("expert")
+    barrier = pltpu.get_barrier_semaphore()
+    for step in range(1, senders):
+        other = lax.rem(me + step, senders)
+        pl.semaphore_signal(barrier, inc=1, device_id={"expert": other}, device_id_type=MESH)
+    pl.semaphore_wait(barrier, senders - 1)
+
+
+def gather_blocks(senders, out, send_sem, recv_sem, visit):
+    depth, z, x, c = place(senders)
+    targets = {
+        UP: lambda: index_of(z + 1, x, c),
+        DOWN: lambda: index_of(z - 1, x, c),
+        ACROSS: lambda: index_of(z, 1 - x, c),
+        SIBLING: lambda: index_of(z, x, 1 - c),
+    }
+
+    def copy(slot, way):
+        return remote(
+            out.at[slot], out.at[slot], send_sem.at[slot, way], recv_sem.at[slot], targets[way]()
+        )
+
+    def arrived(slot):
+        copy(slot, ACROSS).wait_recv()
+
+    def send_on(zb, act):
+        slot = index_of(zb, x, c)
+        pl.when((zb <= z) & (z < depth - 1))(lambda: act(copy(slot, UP)))
+        pl.when((zb >= z) & (z > 0))(lambda: act(copy(slot, DOWN)))
+        act(copy(slot, ACROSS))
+        act(copy(slot, SIBLING))
+
+    def layer(q):
+        return z + (q + 1) // 2 * (2 * (q % 2) - 1)
+
+    def valid(q):
+        return (layer(q) >= 0) & (layer(q) < depth) & (q < 2 * depth - 1)
+
+    send_on(z, lambda one: one.start())
+
+    @pl.loop(0, 2 * depth - 1)
+    def _(q):
+        @pl.when(valid(q + 1))
+        def _():
+            arrived(index_of(layer(q + 1), x, c))
+            send_on(layer(q + 1), lambda one: one.start())
+
+        @pl.when(valid(q))
+        def _():
+            zb = layer(q)
+            slot = index_of(zb, 1 - x, c)
+            arrived(slot)
+            copy(slot, SIBLING).start()
+
+            @pl.loop(0, 2)
+            def _(turn):
+                xb = x + turn * (1 - 2 * x)
+                arrived(index_of(zb, xb, 1 - c))
+                visit(zb, xb)
+
+    @pl.loop(0, depth)
+    def _(zb):
+        send_on(zb, lambda one: one.wait_send())
+        copy(index_of(zb, 1 - x, c), SIBLING).wait_send()
+
+
+def column_of(row):
+    size = row.shape[1]
+    square = (size, size)
+    diagonal = lax.broadcasted_iota(jnp.int32, square, 0) == lax.broadcasted_iota(
+        jnp.int32, square, 1
+    )
+    return jnp.sum(jnp.where(diagonal, row, 0.0), axis=1, keepdims=True)
+
+
+def row_of(column):
+    size = column.shape[0]
+    square = (size, size)
+    diagonal = lax.broadcasted_iota(jnp.int32, square, 0) == lax.broadcasted_iota(
+        jnp.int32, square, 1
+    )
+    return jnp.sum(jnp.where(diagonal, column, 0.0), axis=0, keepdims=True)
+
+
+def product(left, right, left_dim, right_dim):
+    return lax.dot_general(
+        left, right, (((left_dim,), (right_dim,)), ((), ())), preferred_element_type=jnp.float32
+    )
+
+
+def layer_kernel(
+    senders,
+    row_ref,
+    weight_ref,
+    judge_ref,
+    gate_ref,
+    up_ref,
+    down_ref,
+    mixture_ref,
+    inner_ref,
+    grad_gate_ref,
+    grad_up_ref,
+    grad_down_ref,
+    rows,
+    weights,
+    part_ref,
+    expert_out,
+    hidden_all,
+    gate_factor,
+    up_factor,
+    residual,
+    inner_out,
+    sums,
+    sib_in,
+    x_out,
+    x_in,
+    z_out,
+    up_in,
+    down_in,
+    out_total,
+    sib_send,
+    sib_recv,
+    x_send,
+    x_recv,
+    z_send,
+    up_recv,
+    down_recv,
+    row_send,
+    row_recv,
+    residual_send,
+    residual_recv,
+    weight_send,
+    weight_recv,
+    inner_send,
+    inner_recv,
+):
+    me = lax.axis_index("expert")
+    depth, z, x, c = place(senders)
+    tokens, dim_model = row_ref.shape
+    rows[me] = row_ref[...]
+    weights[me] = weight_ref[me]
+    greet_all(senders)
+
+    def to_each(src, dst, send, recv, act):
+        @pl.loop(1, senders)
+        def _(step):
+            other = lax.rem(me + step, senders)
+            act(src, dst, send, recv, other)
+
+    def start_one(src, dst, send, recv, other):
+        remote(src.at[other], dst.at[me], send.at[other], recv.at[me], other).start()
+
+    def land_one(src, dst, send, recv, other):
+        remote(src.at[other], dst.at[other], send.at[other], recv.at[other], other).wait_recv()
+
+    def sent_one(src, dst, send, recv, other):
+        remote(src.at[other], dst.at[me], send.at[other], recv.at[me], other).wait_send()
+
+    weight_way = (weight_ref, weights, weight_send, weight_recv)
+    inner_way = (inner_out, inner_ref, inner_send, inner_recv)
+    to_each(*weight_way, start_one)
+
+    def by_distance(act):
+        for d in range(depth - 1, 0, -1):
+            pl.when(z + d < depth)(functools.partial(act, z + d, UP))
+            pl.when(z - d >= 0)(functools.partial(act, z - d, DOWN))
+        act(z, None)
+
+    def sib_copy(zb, xb):
+        slot = zb * 2 + xb
+        return remote(
+            part_ref.at[index_of(zb, xb, 1 - c)],
+            sib_in.at[slot],
+            sib_send.at[slot],
+            sib_recv.at[slot],
+            index_of(z, x, 1 - c),
+        )
+
+    def x_copy(zb):
+        return remote(
+            x_out.at[zb], x_in.at[zb], x_send.at[zb], x_recv.at[zb], index_of(z, 1 - x, c)
+        )
+
+    def up_copy(zb):
+        return remote(
+            z_out.at[zb], up_in.at[zb], z_send.at[zb], up_recv.at[zb], index_of(z + 1, x, c)
+        )
+
+    def down_copy(zb):
+        return remote(
+            z_out.at[zb], down_in.at[zb], z_send.at[zb], down_recv.at[zb], index_of(z - 1, x, c)
+        )
+
+    def pair(ref, zb, xb):
+        first = index_of(zb, xb, 0)
+        return jnp.concatenate([ref[first], ref[first + 1]], axis=0)
+
+    def pair_weights(zb, xb):
+        first = index_of(zb, xb, 0)
+        return jnp.concatenate(
+            [column_of(weights[first][:1]), column_of(weights[first + 1][:1])], axis=0
+        )
+
+    def forward(zb, xb):
+        first, at = index_of(zb, xb, 0), zb * 2 + xb
+        for core in range(2):
+
+            @pl.when(first + core != me)
+            def _():
+                land_one(*weight_way, first + core)
+
+        block = pair(rows, zb, xb)
+        gate_pre = product(block, gate_ref[0], 1, 1)
+        up_pre = product(block, up_ref[0], 1, 1)
+        sig_gate = jax.nn.sigmoid(gate_pre)
+        silu = gate_pre * sig_gate
+        hidden = (silu * up_pre).astype(jnp.bfloat16)
+        hidden_all[at] = hidden
+        up_factor[at] = silu
+        gate_factor[at] = up_pre * sig_gate * (1.0 + gate_pre * (1.0 - sig_gate))
+        made = product(hidden, down_ref[0], 1, 0).astype(jnp.bfloat16)
+        weighted = (pair_weights(zb, xb) * made.astype(jnp.float32)).astype(jnp.bfloat16)
+        for core in range(2):
+            expert_out[first + core] = made[core * tokens : (core + 1) * tokens]
+            part_ref[first + core] = weighted[core * tokens : (core + 1) * tokens]
+        sib_copy(zb, xb).start()
+
+    def pair_sum(zb, xb):
+        mine = part_ref[index_of(zb, xb, c)].astype(jnp.float32)
+        return mine + sib_in[zb * 2 + xb].astype(jnp.float32)
+
+    def send_across(zb, way):
+        sib_copy(zb, 1 - x).wait_recv()
+        x_out[zb] = pair_sum(zb, 1 - x).astype(jnp.bfloat16)
+        x_copy(zb).start()
+
+    def send_along(zb, way):
+        sib_copy(zb, x).wait_recv()
+        x_copy(zb).wait_recv()
+        out_total[...] = pair_sum(zb, x) + x_in[zb].astype(jnp.float32)
+        if way != DOWN:
+
+            @pl.when(z > 0)
+            def _():
+                up_copy(zb).wait_recv()
+                out_total[...] += up_in[zb].astype(jnp.float32)
+
+        if way != UP:
+
+            @pl.when(z < depth - 1)
+            def _():
+                down_copy(zb).wait_recv()
+                out_total[...] += down_in[zb].astype(jnp.float32)
+
+        if way is not None:
+            z_out[zb] = out_total[...].astype(jnp.bfloat16)
+            (up_copy if way == UP else down_copy)(zb).start()
+
+    def finish(zb, way):
+        sib_copy(zb, 1 - x).wait_send()
+        sib_copy(zb, x).wait_send()
+        x_copy(zb).wait_send()
+        if way is not None:
+            (up_copy if way == UP else down_copy)(zb).wait_send()
+
+    def backward(zb, xb):
+        first, at = index_of(zb, xb, 0), zb * 2 + xb
+        wide = pair(residual, zb, xb).astype(jnp.float32)
+        out_grad = (pair_weights(zb, xb) * wide).astype(jnp.bfloat16)
+        inner = jnp.sum(pair(expert_out, zb, xb).astype(jnp.float32) * wide, axis=1, keepdims=True)
+        for core in range(2):
+            line = row_of(inner[core * tokens : (core + 1) * tokens])
+            inner_out[first + core] = jnp.broadcast_to(line, inner_out.shape[1:])
+
+            @pl.when(first + core != me)
+            def _():
+                start_one(*inner_way, first + core)
+
+        hidden_grad = product(out_grad, down_ref[0], 1, 1)
+        gate_grad = (hidden_grad * gate_factor[at]).astype(jnp.bfloat16)
+        up_grad = (hidden_grad * up_factor[at]).astype(jnp.bfloat16)
+        block = pair(rows, zb, xb)
+        sums[0] += product(gate_grad, block, 0, 0)
+        sums[1] += product(up_grad, block, 0, 0)
+        sums[2] += product(hidden_all[at], out_grad, 0, 0)
+
+    gather_blocks(senders, rows, row_send, row_recv, forward)
+    by_distance(send_across)
+    by_distance(send_along)
+    mixture = out_total[...]
+    mixture_ref[...] = mixture.astype(jnp.bfloat16)
+    residual[me] = (mixture - judge_ref[...].astype(jnp.float32)).astype(jnp.bfloat16)
+    sums[...] = jnp.zeros_like(sums)
+    gather_blocks(senders, residual, residual_send, residual_recv, backward)
+    inner_ref[me] = inner_out[me]
+    grad_gate_ref[0] = sums[0].astype(jnp.bfloat16)
+    grad_up_ref[0] = sums[1].astype(jnp.bfloat16)
+    grad_down_ref[0] = sums[2].astype(jnp.bfloat16)
+    by_distance(finish)
+    to_each(*weight_way, sent_one)
+    to_each(*inner_way, land_one)
+    to_each(*inner_way, sent_one)
+
+
+def vmem_specs(count):
+    return [pl.BlockSpec(memory_space=pltpu.VMEM)] * count
+
+
+def whole_layer(rows, weights, judge, w_gate, w_up, w_down):
+    senders = weights.shape[0]
+    depth = senders // 4
+    pairs = senders // 2
+    block = rows.shape
+    tokens = block[0]
+    units = w_gate.shape[1]
+    dma = pltpu.SemaphoreType.DMA
+
+    def blocks(count):
+        return pltpu.VMEM((count, *block), jnp.bfloat16)
+
+    def unit_blocks(dtype):
+        return pltpu.VMEM((pairs, 2 * tokens, units), dtype)
+
+    grad = jax.ShapeDtypeStruct(w_gate.shape, jnp.bfloat16)
+    return pl.pallas_call(
+        functools.partial(layer_kernel, senders),
+        out_shape=(
+            jax.ShapeDtypeStruct(block, jnp.bfloat16),
+            jax.ShapeDtypeStruct(weights.shape, weights.dtype),
+            grad,
+            grad,
+            grad,
+        ),
+        in_specs=vmem_specs(6),
+        out_specs=tuple(vmem_specs(5)),
+        scratch_shapes=[
+            blocks(senders),
+            pltpu.VMEM(weights.shape, weights.dtype),
+            blocks(senders),
+            blocks(senders),
+            unit_blocks(jnp.bfloat16),
+            unit_blocks(jnp.float32),
+            unit_blocks(jnp.float32),
+            blocks(senders),
+            pltpu.VMEM(weights.shape, weights.dtype),
+            pltpu.VMEM((3, *w_gate.shape[1:]), jnp.float32),
+            blocks(2 * depth),
+            blocks(depth),
+            blocks(depth),
+            blocks(depth),
+            blocks(depth),
+            blocks(depth),
+            pltpu.VMEM(block, jnp.float32),
+            dma((2 * depth,)),
+            dma((2 * depth,)),
+            dma((depth,)),
+            dma((depth,)),
+            dma((depth,)),
+            dma((depth,)),
+            dma((depth,)),
+            dma((senders, 4)),
+            dma((senders,)),
+            dma((senders, 4)),
+            dma((senders,)),
+            dma((senders,)),
+            dma((senders,)),
+            dma((senders,)),
+            dma((senders,)),
+        ],
+        compiler_params=pltpu.CompilerParams(
+            collective_id=0, has_side_effects=True, vmem_limit_bytes=56 << 20
+        ),
+    )(rows, weights, judge, w_gate, w_up, w_down)
+
+
+def dense_rows(student_input, judge_output, expert_ids, route_weights, w_gate, w_up, w_down):
+    experts = lax.axis_size("expert")
+    tok_count = student_input.shape[0]
+    chosen = expert_ids[:, :, None] == jnp.arange(experts, dtype=jnp.int32)[None, None, :]
+    dense_weights = jnp.sum(jnp.where(chosen, route_weights[:, :, None], 0.0), axis=1)
+    lines = jnp.broadcast_to(dense_weights.T[:, None, :], (experts, 8, tok_count))
+    mixture, inner, *grads = whole_layer(student_input, lines, judge_output, w_gate, w_up, w_down)
+    route_grads = jnp.sum(jnp.where(chosen, inner[:, 0].T[:, None, :], 0.0), axis=2)
+    return (mixture, route_grads, *grads)
+
+
+def on_device(student_input, judge_output, expert_ids, route_weights, w_gate, w_up, w_down):
+    experts = w_gate.shape[0] * lax.axis_size("expert")
+    senders = lax.axis_size("expert")
+    alone = w_gate.shape[0] == 1 and lax.axis_size("dp") == 1 and senders % 4 == 0
+    dense = alone and experts <= 4 * expert_ids.shape[1]
+    form = dense_rows if dense else routed_rows
+    return form(student_input, judge_output, expert_ids, route_weights, w_gate, w_up, w_down)
+
+
 def solution(mesh):
     placed = (
         P(("groups", "dp", "expert"), None),

time: 292 us -> 133 us (0.46)
  the two profiles are of different devices: /device:TPU:11 before, /device:TPU:0 now
where the time goes in v3:
time: 133 us; the launch traced here: 132 us
  Pallas kernels  123 us (92%)
  local copies, waits for them, and re-layouts  7.59 us (6%)
  other arithmetic  1.33 us (1%)
    pallas_call x1, Pallas kernels, whole_layer(): pl.pallas_call(functools.partial(layer_kernel, senders), out_shape=(jax.S...  123 us
    unnamed x10, local copies, waits for them, and re-layouts  6.11 us

profile of v3, /device:TPU:0, one launch (start us, length us, event | category | flops | bytes accessed | tf_op | source)
XLA Modules:
  0.0 132.3 jit_solution(2767315819184944924)
XLA Ops:
  0.6 0.7 select_reduce_fusion.1
  1.4 0.6 broadcast_in_dim.34.weight_ref
  2.0 0.0 copy-start.2
  2.0 122.7 %shard_map.110 = (bf16[128,1024]{1,0:T(8,128)(2,1)}, f32[16,8,128]{2,1,0:T(8,128)}, bf16[1,384,1024]{2,1,0:T(8,128)(2,1)}, bf16[1,384,1024]{2,1,0:T(8,128)(2,1)}, bf16[1,384,1024]{2,1,0:T(8,128)(2,1)}) custom-call(bf16[128,1024]{1,0:T(8,128)(2,1)} %row_ref.1, f32[16,8,128]{2,1,0:T(8,128)} %broadcast_in_dim.34.weight_ref, bf16[128,1024]{1,0:T(8,128)(2,1)} %judge_ref.1, ...), custom_call_target="tpu_custom_call" | custom-call | tf_op jit(solution)/shard_map/pallas_call | solution.py:467
  124.7 0.8 slice.3
  125.5 0.0 copy-done.2
  125.5 0.6 select_reduce_fusion
  126.2 1.7 %copy.19 = bf16[128,1024]{1,0:T(8,128)(2,1)} copy(bf16[128,1024]{1,0:T(8,128)(2,1)} %get-tuple-element.20) | data formatting | bytes 524288
  127.8 0.0 copy-start.1
  127.8 2.1 %copy.20 = bf16[1,384,1024]{2,1,0:T(8,128)(2,1)} copy(bf16[1,384,1024]{2,1,0:T(8,128)(2,1)} %get-tuple-element.22) | data formatting | bytes 1572864
  130.0 0.0 copy-done.1
  130.0 0.0 copy-start
  130.0 0.9 copy.21
  130.8 0.5 copy-done
  131.4 0.9 copy.22
Async XLA Ops:
  2.0 123.6 %copy-start.2 = (s32[128,8]{0,1:T(8,128)S(1)}, s32[128,8]{0,1:T(8,128)}, u32[]{:S(2)}) copy-start(s32[128,8]{0,1:T(8,128)} %param.9) | copy-start | bytes 12292
  127.8 2.1 %copy-start.1 = (bf16[1,384,1024]{2,1,0:T(8,128)(2,1)S(1)}, bf16[1,384,1024]{2,1,0:T(8,128)(2,1)}, u32[]{:S(2)}) copy-start(bf16[1,384,1024]{2,1,0:T(8,128)(2,1)} %get-tuple-element.23) | copy-start | bytes 2359300
  130.0 1.4 %copy-start = (bf16[1,384,1024]{2,1,0:T(8,128)(2,1)S(1)}, bf16[1,384,1024]{2,1,0:T(8,128)(2,1)}, u32[]{:S(2)}) copy-start(bf16[1,384,1024]{2,1,0:T(8,128)(2,1)} %get-tuple-element.24) | copy-start | bytes 2359300

commit v4 on v3

--- a/solution.py
+++ b/solution.py
@@ -172,33 +172,37 @@
         act(copy(slot, ACROSS))
         act(copy(slot, SIBLING))
 
-    def layer(q):
-        return z + (q + 1) // 2 * (2 * (q % 2) - 1)
-
-    def valid(q):
-        return (layer(q) >= 0) & (layer(q) < depth) & (q < 2 * depth - 1)
+    near = jnp.minimum(z, depth - 1 - z)
+
+    def layer(p):
+        both_sides = z + (p + 1) // 2 * (1 - 2 * (p % 2))
+        one_side = jnp.where(z < depth - 1 - z, p, depth - 1 - p)
+        return jnp.where(p <= 2 * near, both_sides, one_side)
+
+    def column_arrival(p):
+        zb = layer(p)
+        arrived(index_of(zb, x, c))
+        send_on(zb, lambda one: one.start())
 
     send_on(z, lambda one: one.start())
 
-    @pl.loop(0, 2 * depth - 1)
-    def _(q):
-        @pl.when(valid(q + 1))
+    @pl.loop(0, 2 * depth)
+    def _(step):
+        p = step // 2
+        turn = step % 2
+        zb = layer(p)
+
+        @pl.when(turn == 1)
         def _():
-            arrived(index_of(layer(q + 1), x, c))
-            send_on(layer(q + 1), lambda one: one.start())
-
-        @pl.when(valid(q))
-        def _():
-            zb = layer(q)
+            pl.when(p == 0)(lambda: column_arrival(1))
+            pl.when(p + 2 < depth)(lambda: column_arrival(p + 2))
             slot = index_of(zb, 1 - x, c)
             arrived(slot)
             copy(slot, SIBLING).start()
 
-            @pl.loop(0, 2)
-            def _(turn):
-                xb = x + turn * (1 - 2 * x)
-                arrived(index_of(zb, xb, 1 - c))
-                visit(zb, xb)
+        xb = x + turn * (1 - 2 * x)
+        arrived(index_of(zb, xb, 1 - c))
+        visit(zb, xb)
 
     @pl.loop(0, depth)
     def _(zb):
@@ -529,7 +533,7 @@
 def on_device(student_input, judge_output, expert_ids, route_weights, w_gate, w_up, w_down):
     experts = w_gate.shape[0] * lax.axis_size("expert")
     senders = lax.axis_size("expert")
-    alone = w_gate.shape[0] == 1 and lax.axis_size("dp") == 1 and senders % 4 == 0
+    alone = w_gate.shape[0] == 1 and lax.axis_size("dp") == 1 and senders % 4 == 0 and senders > 4
     dense = alone and experts <= 4 * expert_ids.shape[1]
     form = dense_rows if dense else routed_rows
     return form(student_input, judge_output, expert_ids, route_weights, w_gate, w_up, w_down)

time: 133 us -> 119 us (0.89)
  Pallas kernels: 123 us -> 109 us
    pallas_call x1, Pallas kernels: 123 us -> 109 us  [whole_layer(): pl.pallas_call(functools.partial(layer_kernel, senders), out_shape=(jax.S...]
where the time goes in v4:
time: 119 us; the launch traced here: 118 us
  Pallas kernels  109 us (92%)
  local copies, waits for them, and re-layouts  7.59 us (6%)
  other arithmetic  1.33 us (1%)
    pallas_call x1, Pallas kernels, whole_layer(): pl.pallas_call(functools.partial(layer_kernel, senders), out_shape=(jax.S...  109 us
    unnamed x10, local copies, waits for them, and re-layouts  6.11 us

profile of v4, /device:TPU:0, one launch (start us, length us, event | category | flops | bytes accessed | tf_op | source)
XLA Modules:
  0.0 118.4 jit_solution(4058770756411776581)
XLA Ops:
  0.6 0.7 select_reduce_fusion.1
  1.4 0.6 broadcast_in_dim.34.weight_ref
  2.0 0.0 copy-start.2
  2.0 108.8 %shard_map.110 = (bf16[128,1024]{1,0:T(8,128)(2,1)}, f32[16,8,128]{2,1,0:T(8,128)}, bf16[1,384,1024]{2,1,0:T(8,128)(2,1)}, bf16[1,384,1024]{2,1,0:T(8,128)(2,1)}, bf16[1,384,1024]{2,1,0:T(8,128)(2,1)}) custom-call(bf16[128,1024]{1,0:T(8,128)(2,1)} %row_ref.1, f32[16,8,128]{2,1,0:T(8,128)} %broadcast_in_dim.34.weight_ref, bf16[128,1024]{1,0:T(8,128)(2,1)} %judge_ref.1, ...), custom_call_target="tpu_custom_call" | custom-call | tf_op jit(solution)/shard_map/pallas_call | solution.py:471
  110.8 0.8 slice.3
  111.7 0.0 copy-done.2
  111.7 0.6 select_reduce_fusion
  112.3 1.7 %copy.19 = bf16[128,1024]{1,0:T(8,128)(2,1)} copy(bf16[128,1024]{1,0:T(8,128)(2,1)} %get-tuple-element.20) | data formatting | bytes 524288
  114.0 0.0 copy-start.1
  114.0 2.1 %copy.20 = bf16[1,384,1024]{2,1,0:T(8,128)(2,1)} copy(bf16[1,384,1024]{2,1,0:T(8,128)(2,1)} %get-tuple-element.22) | data formatting | bytes 1572864
  116.1 0.0 copy-done.1
  116.1 0.0 copy-start
  116.1 0.9 copy.21
  117.0 0.5 copy-done
  117.5 0.9 copy.22
Async XLA Ops:
  2.0 109.7 %copy-start.2 = (s32[128,8]{0,1:T(8,128)S(1)}, s32[128,8]{0,1:T(8,128)}, u32[]{:S(2)}) copy-start(s32[128,8]{0,1:T(8,128)} %param.9) | copy-start | bytes 12292
  114.0 2.1 %copy-start.1 = (bf16[1,384,1024]{2,1,0:T(8,128)(2,1)S(1)}, bf16[1,384,1024]{2,1,0:T(8,128)(2,1)}, u32[]{:S(2)}) copy-start(bf16[1,384,1024]{2,1,0:T(8,128)(2,1)} %get-tuple-element.23) | copy-start | bytes 2359300
  116.1 1.4 %copy-start = (bf16[1,384,1024]{2,1,0:T(8,128)(2,1)S(1)}, bf16[1,384,1024]{2,1,0:T(8,128)(2,1)}, u32[]{:S(2)}) copy-start(bf16[1,384,1024]{2,1,0:T(8,128)(2,1)} %get-tuple-element.24) | copy-start | bytes 2359300

commit v5 on v4

--- a/solution.py
+++ b/solution.py
@@ -432,11 +432,11 @@
 
     gather_blocks(senders, rows, row_send, row_recv, forward)
     by_distance(send_across)
+    sums[...] = jnp.zeros_like(sums)
     by_distance(send_along)
     mixture = out_total[...]
     mixture_ref[...] = mixture.astype(jnp.bfloat16)
     residual[me] = (mixture - judge_ref[...].astype(jnp.float32)).astype(jnp.bfloat16)
-    sums[...] = jnp.zeros_like(sums)
     gather_blocks(senders, residual, residual_send, residual_recv, backward)
     inner_ref[me] = inner_out[me]
     grad_gate_ref[0] = sums[0].astype(jnp.bfloat16)
@@ -519,6 +519,22 @@
     )(rows, weights, judge, w_gate, w_up, w_down)
 
 
+def hand_on(*arrays):
+    count = len(arrays)
+
+    def kernel(*refs):
+        for src, dst in zip(refs[:count], refs[count:]):
+            dst[...] = src[...]
+
+    return pl.pallas_call(
+        kernel,
+        out_shape=tuple(jax.ShapeDtypeStruct(a.shape, a.dtype) for a in arrays),
+        in_specs=vmem_specs(count),
+        out_specs=tuple(vmem_specs(count)),
+        compiler_params=pltpu.CompilerParams(vmem_limit_bytes=16 << 20),
+    )(*arrays)
+
+
 def dense_rows(student_input, judge_output, expert_ids, route_weights, w_gate, w_up, w_down):
     experts = lax.axis_size("expert")
     tok_count = student_input.shape[0]
@@ -527,6 +543,7 @@
     lines = jnp.broadcast_to(dense_weights.T[:, None, :], (experts, 8, tok_count))
     mixture, inner, *grads = whole_layer(student_input, lines, judge_output, w_gate, w_up, w_down)
     route_grads = jnp.sum(jnp.where(chosen, inner[:, 0].T[:, None, :], 0.0), axis=2)
+    mixture, *grads = hand_on(mixture, *grads)
     return (mixture, route_grads, *grads)
 
 

time: 119 us -> 119 us (level)
  local copies, waits for them, and re-layouts: 7.59 us -> 5.82 us
    unnamed x10, local copies, waits for them, and re-layouts: 6.11 us -> 4.34 us
    pallas_call x0 -> x1, Pallas kernels: none -> 1.65 us  [hand_on(): pl.pallas_call(kernel, out_shape=tuple((jax.ShapeDtypeStruct(a.shape, a.d...]
where the time goes in v5:
time: 119 us; the launch traced here: 118 us
  Pallas kernels  110 us (92%)
  local copies, waits for them, and re-layouts  5.82 us (5%)
  other arithmetic  1.33 us (1%)
    pallas_call x1, Pallas kernels, whole_layer(): pl.pallas_call(functools.partial(layer_kernel, senders), out_shape=(jax.S...  109 us
    unnamed x10, local copies, waits for them, and re-layouts  4.34 us

profile of v5, /device:TPU:0, one launch (start us, length us, event | category | flops | bytes accessed | tf_op | source)
XLA Modules:
  0.0 118.3 jit_solution(11640366612888759933)
XLA Ops:
  0.6 0.7 select_reduce_fusion.1
  1.4 0.6 broadcast_in_dim.34.weight_ref
  2.0 108.8 %shard_map.110 = (bf16[128,1024]{1,0:T(8,128)(2,1)}, f32[16,8,128]{2,1,0:T(8,128)}, bf16[1,384,1024]{2,1,0:T(8,128)(2,1)}, bf16[1,384,1024]{2,1,0:T(8,128)(2,1)}, bf16[1,384,1024]{2,1,0:T(8,128)(2,1)}) custom-call(bf16[128,1024]{1,0:T(8,128)(2,1)} %row_ref.1, f32[16,8,128]{2,1,0:T(8,128)} %broadcast_in_dim.34.weight_ref, bf16[128,1024]{1,0:T(8,128)(2,1)} %judge_ref.1, ...), custom_call_target="tpu_custom_call" | custom-call | tf_op jit(solution)/shard_map/pallas_call | solution.py:471
  110.8 0.0 copy-start
  110.9 1.1 copy-done
  112.0 0.0 copy-start.1
  112.0 1.1 copy-done.1
  113.1 0.0 copy-start.2
  113.1 1.1 copy-done.2
  114.2 0.0 copy-start.3
  114.2 0.9 copy-done.3
  115.2 0.0 copy-start.4
  115.2 1.7 %shard_map.111 = (bf16[128,1024]{1,0:T(8,128)(2,1)}, bf16[1,384,1024]{2,1,0:T(8,128)(2,1)}, bf16[1,384,1024]{2,1,0:T(8,128)(2,1)}, bf16[1,384,1024]{2,1,0:T(8,128)(2,1)}) custom-call(bf16[128,1024]{1,0:T(8,128)(2,1)S(1)} %copy-done.3, bf16[1,384,1024]{2,1,0:T(8,128)(2,1)S(1)} %copy-done, bf16[1,384,1024]{2,1,0:T(8,128)(2,1)S(1)} %copy-done.1, ...), custom_call_target="tpu_custom_call" | custom-call | tf_op jit(solution)/shard_map/pallas_call | solution.py:529
  116.8 0.8 slice.3
  117.7 0.0 copy-done.4
  117.7 0.6 select_reduce_fusion
Async XLA Ops:
  110.8 1.1 copy-start
  112.0 1.1 copy-start.1
  113.1 1.1 copy-start.2
  114.2 0.9 copy-start.3
  115.2 2.5 %copy-start.4 = (s32[128,8]{0,1:T(8,128)S(1)}, s32[128,8]{0,1:T(8,128)}, u32[]{:S(2)}) copy-start(s32[128,8]{0,1:T(8,128)} %param.9) | copy-start | bytes 12292

commit v6 on v5

--- a/solution.py
+++ b/solution.py
@@ -523,15 +523,21 @@
     count = len(arrays)
 
     def kernel(*refs):
-        for src, dst in zip(refs[:count], refs[count:]):
-            dst[...] = src[...]
+        done = refs[-1]
+        copies = [
+            pltpu.make_async_copy(refs[i], refs[count + i], done.at[i]) for i in range(count)
+        ]
+        for one in copies:
+            one.start()
+        for one in copies:
+            one.wait()
 
     return pl.pallas_call(
         kernel,
         out_shape=tuple(jax.ShapeDtypeStruct(a.shape, a.dtype) for a in arrays),
-        in_specs=vmem_specs(count),
-        out_specs=tuple(vmem_specs(count)),
-        compiler_params=pltpu.CompilerParams(vmem_limit_bytes=16 << 20),
+        in_specs=[pl.BlockSpec(memory_space=pl.ANY)] * count,
+        out_specs=(pl.BlockSpec(memory_space=pl.ANY),) * count,
+        scratch_shapes=[pltpu.SemaphoreType.DMA((count,))],
     )(*arrays)
 
 

time: 119 us -> 193 us (1.62)
  Pallas kernels: 110 us -> 189 us
  local copies, waits for them, and re-layouts: 5.82 us -> 1.49 us
    pallas_call x1, Pallas kernels: 1.65 us -> 80.5 us  [hand_on(): pl.pallas_call(kernel, out_shape=tuple((jax.ShapeDtypeStruct(a.shape, a.d...]
    unnamed x10 -> x2, local copies, waits for them, and re-layouts: 4.34 us -> 0.01 us
where the time goes in v6:
time: 193 us
  Pallas kernels  189 us (98%)
    pallas_call x1, Pallas kernels, whole_layer(): pl.pallas_call(functools.partial(layer_kernel, senders), out_shape=(jax.S...  109 us
    pallas_call x1, Pallas kernels, hand_on(): pl.pallas_call(kernel, out_shape=tuple((jax.ShapeDtypeStruct(a.shape, a.d...  80.5 us

profile of v6, /device:TPU:0, one launch (start us, length us, event | category | flops | bytes accessed | tf_op | source)
XLA Modules:
  0.0 192.9 jit_solution(10478006609891323479)
XLA Ops:
  0.6 0.7 select_reduce_fusion.1
  1.4 0.6 broadcast_in_dim.34.weight_ref
  2.0 108.9 %shard_map.110 = (bf16[128,1024]{1,0:T(8,128)(2,1)}, f32[16,8,128]{2,1,0:T(8,128)}, bf16[1,384,1024]{2,1,0:T(8,128)(2,1)}, bf16[1,384,1024]{2,1,0:T(8,128)(2,1)}, bf16[1,384,1024]{2,1,0:T(8,128)(2,1)}) custom-call(bf16[128,1024]{1,0:T(8,128)(2,1)} %row_ref.1, f32[16,8,128]{2,1,0:T(8,128)} %broadcast_in_dim.34.weight_ref, bf16[128,1024]{1,0:T(8,128)(2,1)} %judge_ref.1, ...), custom_call_target="tpu_custom_call" | custom-call | tf_op jit(solution)/shard_map/pallas_call | solution.py:471
  110.9 0.0 copy-start
  110.9 80.5 %shard_map.111 = (bf16[128,1024]{1,0:T(8,128)(2,1)}, bf16[1,384,1024]{2,1,0:T(8,128)(2,1)}, bf16[1,384,1024]{2,1,0:T(8,128)(2,1)}, bf16[1,384,1024]{2,1,0:T(8,128)(2,1)}) custom-call(bf16[128,1024]{1,0:T(8,128)(2,1)} %get-tuple-element.14.refs_0_, bf16[1,384,1024]{2,1,0:T(8,128)(2,1)} %get-tuple-element.15.refs_1_, ...), custom_call_target="tpu_custom_call" | custom-call | tf_op jit(solution)/shard_map/pallas_call | solution.py:535
  191.4 0.8 slice.3
  192.3 0.0 copy-done
  192.3 0.6 select_reduce_fusion
Async XLA Ops:
  110.9 81.4 %copy-start = (s32[128,8]{0,1:T(8,128)S(1)}, s32[128,8]{0,1:T(8,128)}, u32[]{:S(2)}) copy-start(s32[128,8]{0,1:T(8,128)} %param.9) | copy-start | bytes 12292
